TPU v7x, 128 devices: a whole 4x4x4 slice. The times are simulated.
128 devices in a mesh: gx: 8 (over z, x_hi), gy: 16 (over x_lo, y, core).
Axes of the slice: x: 4 (x_hi: 2, x_lo: 2; x = x_hi * 2 + x_lo), y: 4, z: 4, core: 2. Of those that a mesh axis runs over, the one named last changes fastest.
Arguments:
- efield: float32 [3, 256, 512, 128], P(None, 'gx', 'gy'), may hold values from -6 to 6
- hfield: float32 [3, 256, 512, 128], P(None, 'gx', 'gy'), may hold values from -6 to 6
- e_coef: float32 [256, 512, 128], P('gx', 'gy'), may hold values from 0.2 to 0.6
- omega: float32 [4], replicated, may hold values from 0.1 to 0.8
- patch_owner: int32 [128], replicated, may hold values from 0 to 127, as said below
- patch_corner: int32 [128, 2], replicated, may hold values from 1 to 23
- surface_points: int32 [8, 16, 256], P('gx', 'gy'), may hold values from -1 to 131071, as said below
- surface_faces: int32 [8, 16, 256], P('gx', 'gy'), may hold values from 0 to 5, as said below
- angle_index: int32 [4096, 2], replicated, may hold values from 0 to 127
Outputs:
- efield_out: float32 [3, 256, 512, 128], P(None, 'gx', 'gy')
- hfield_out: float32 [3, 256, 512, 128], P(None, 'gx', 'gy')
- far_field: float32 [4096, 48], P(('gx', 'gy'))
Inputs may be any that keep to these rules, and one draw needn't show every extreme that they name: `patch_owner`: every device index appears at most 4 times, and some device exactly 4 times. `surface_points`: the points lie on the faces of the box of cells 32 // 2 to 239, 16 to 495 and 16 to 111, each on the face named by surface_faces. A block's live slots come first and the rest hold -1; the number live in a block is proportional to the box-face area inside it, and the fullest block has all 256 live. `surface_faces`: empty slots hold 0. `angle_index`: the azimuthal index is below 128.
All inputs are finite; a program needn't handle non-finite values.
Results may differ from a plain program's by a relative error of at most 0.0003.
Values sent between devices are 32-bit elements; how exact they have to be, the bound alone decides.
A program may use at most 320 MiB of HBM per device.

v0:
```python
import math

import jax
import jax.numpy as jnp
from jax import lax
from jax.sharding import PartitionSpec as P

PB = 8
SLOTS = 4
STEPS = 2
NTH = 128
NPH = 256


H_COEF = 0.5


def passed_along(block, axis, distance):
    devices = range(lax.axis_size(axis))
    route = [(i - distance, i) for i in devices if i - distance in devices]
    return lax.ppermute(block, axis, route)


def forward(field, axis, edge):
    after = jnp.concatenate(
        [lax.slice_in_dim(field, 1, field.shape[axis], axis=axis), edge], axis=axis
    )
    return after - field


def backward(field, axis, edge):
    before = jnp.concatenate(
        [edge, lax.slice_in_dim(field, 0, field.shape[axis] - 1, axis=axis)], axis=axis
    )
    return field - before


def zero_edges(field):
    first = field[0]
    x_edge = jnp.zeros((2, 1) + first.shape[1:], first.dtype)
    y_edge = jnp.zeros((2, first.shape[0], 1, first.shape[2]), first.dtype)
    return (x_edge, y_edge)


def curl_forward(efield, x_edge, y_edge):
    if x_edge is None:
        x_edge, y_edge = zero_edges(efield)
    comp_x, comp_y, comp_z = (efield[0], efield[1], efield[2])
    z_edge = jnp.zeros(comp_x.shape[:2] + (1,), comp_x.dtype)
    curl_x = forward(comp_z, 1, y_edge[1]) - forward(comp_y, 2, z_edge)
    curl_y = forward(comp_x, 2, z_edge) - forward(comp_z, 0, x_edge[1])
    curl_z = forward(comp_y, 0, x_edge[0]) - forward(comp_x, 1, y_edge[0])
    return jnp.stack([curl_x, curl_y, curl_z])


def curl_backward(hfield, x_edge, y_edge):
    if x_edge is None:
        x_edge, y_edge = zero_edges(hfield)
    comp_x, comp_y, comp_z = (hfield[0], hfield[1], hfield[2])
    z_edge = jnp.zeros(comp_x.shape[:2] + (1,), comp_x.dtype)
    curl_x = backward(comp_z, 1, y_edge[1]) - backward(comp_y, 2, z_edge)
    curl_y = backward(comp_x, 2, z_edge) - backward(comp_z, 0, x_edge[1])
    curl_z = backward(comp_y, 0, x_edge[0]) - backward(comp_x, 1, y_edge[0])
    return jnp.stack([curl_x, curl_y, curl_z])


def refine(efield, hfield, e_coef, x_start, y_start):
    span = PB + 2
    depth = efield.shape[3]
    anchor = jnp.zeros((), jnp.int32)
    hp = lax.Precision.HIGHEST
    fine_lanes = jnp.arange(2 * depth, dtype=jnp.int32) // 2
    spread = (jnp.arange(depth, dtype=jnp.int32)[:, None] == fine_lanes[None, :]).astype(
        jnp.float32
    )
    halving = spread.T * 0.5

    def cutout(field):
        return lax.dynamic_slice(field, (anchor, x_start, y_start, anchor), (3, span, span, depth))

    def finer(field):
        wider = jnp.repeat(jnp.repeat(field, 2, axis=-3), 2, axis=-2)
        return jnp.dot(wider, spread, precision=hp)

    e_start = finer(cutout(efield))
    h_start = finer(cutout(hfield))
    coef_fine = finer(lax.dynamic_slice(e_coef, (x_start, y_start, anchor), (span, span, depth)))
    lanes = jnp.arange(2 * span)
    inner_line = (lanes >= 2) & (lanes < 2 * span - 2)
    inner = (inner_line[:, None] & inner_line[None, :])[None, :, :, None]
    e_fine, h_fine = (e_start, h_start)
    for substep in range(2):
        h_fine = h_fine - H_COEF * curl_forward(e_fine, None, None)
        e_fine = e_fine + coef_fine * curl_backward(h_fine, None, None)
        e_fine = jnp.where(inner, e_fine, e_start)
        h_fine = jnp.where(inner, h_fine, h_start)

    def coarsen(field):
        core = jnp.dot(field[:, 2:-2, 2:-2, :], halving, precision=hp)
        core = core.reshape(3, PB, 2, PB, 2, depth)
        return jnp.sum(core, axis=(2, 4)) * 0.25

    start = (anchor, x_start + 1, y_start + 1, anchor)
    efield = lax.dynamic_update_slice(efield, coarsen(e_fine), start)
    hfield = lax.dynamic_update_slice(hfield, coarsen(h_fine), start)
    return (efield, hfield)


def face_normals(points, faces):
    live = (points >= 0).astype(jnp.float32)
    axis_num = faces // 2
    sign = (2 * (faces % 2) - 1).astype(jnp.float32)
    return jnp.stack([(axis_num == k).astype(jnp.float32) * sign * live for k in range(3)])


def cross_normal(normals, field):
    return jnp.stack(
        [
            normals[1] * field[2] - normals[2] * field[1],
            normals[2] * field[0] - normals[0] * field[2],
            normals[0] * field[1] - normals[1] * field[0],
        ]
    )


def accumulate(currents, efield, hfield, points, normals, omega, moment):
    e_taken = jnp.take(efield.reshape(3, -1), points, axis=1)
    h_taken = jnp.take(hfield.reshape(3, -1), points, axis=1)
    sampled = jnp.concatenate(
        [cross_normal(normals, h_taken), -cross_normal(normals, e_taken)], axis=0
    )
    cosine = jnp.cos(omega * moment)
    sine = jnp.sin(omega * moment)
    term = jnp.stack(
        [sampled[None] * cosine[:, None, None], -sampled[None] * sine[:, None, None]], axis=1
    )
    return currents + term


def project(angle_rows, omega, currents, positions, scale):
    theta = math.pi * (angle_rows[:, 0].astype(jnp.float32) + 0.5) / NTH
    phi = 2.0 * math.pi * (angle_rows[:, 1].astype(jnp.float32) + 0.5) / NPH
    direction = jnp.stack(
        [jnp.sin(theta) * jnp.cos(phi), jnp.sin(theta) * jnp.sin(phi), jnp.cos(theta)], axis=1
    )
    along = jnp.dot(
        direction, positions, precision=lax.Precision.HIGHEST, preferred_element_type=jnp.float32
    )
    pieces = []
    for freq_num in range(currents.shape[0]):
        phase = omega[freq_num] * along
        cosine = jnp.cos(phase)
        sine = jnp.sin(phase)
        real_cur = currents[freq_num, 0].T
        imag_cur = currents[freq_num, 1].T
        hp = lax.Precision.HIGHEST
        real_part = jnp.dot(cosine, real_cur, precision=hp) - jnp.dot(sine, imag_cur, precision=hp)
        imag_part = jnp.dot(sine, real_cur, precision=hp) + jnp.dot(cosine, imag_cur, precision=hp)
        pieces.append(real_part)
        pieces.append(imag_part)
    return jnp.concatenate(pieces, axis=1) * scale


def project_blocks(angle_rows, omega, currents, positions, scale):
    count = angle_rows.shape[0]
    piece = 512
    blocks = angle_rows.reshape(count // piece, piece, 2)
    result = lax.map(lambda rows: project(rows, omega, currents, positions, scale), blocks)
    return result.reshape(count, result.shape[-1])


def local(
    efield,
    hfield,
    e_coef,
    omega,
    patch_owner,
    patch_corner,
    surface_points,
    surface_faces,
    angle_index,
):
    block = efield.shape[1]
    depth = efield.shape[3]
    width_x = lax.axis_size("gx")
    width_y = lax.axis_size("gy")
    device_num = lax.axis_index(("gx", "gy"))
    mine = (patch_owner == device_num).astype(jnp.int32)
    ranks = jnp.cumsum(mine) - 1
    slot_values = surface_points.reshape(-1)
    normals = face_normals(slot_values, surface_faces.reshape(-1))
    points = jnp.maximum(slot_values, 0)
    currents = jnp.zeros((omega.shape[0], 2, 6, points.shape[0]), jnp.float32)
    for moment in range(STEPS):
        ex_edge = passed_along(efield[1:3, 0:1], "gx", -1)
        ey_edge = passed_along(jnp.stack([efield[0][:, 0:1], efield[2][:, 0:1]]), "gy", -1)
        hfield = hfield - H_COEF * curl_forward(efield, ex_edge, ey_edge)
        hx_edge = passed_along(hfield[1:3, -1:], "gx", 1)
        hy_edge = passed_along(jnp.stack([hfield[0][:, -1:], hfield[2][:, -1:]]), "gy", 1)
        efield = efield + e_coef * curl_backward(hfield, hx_edge, hy_edge)
        for place in range(SLOTS):
            chosen = mine * (ranks == place).astype(jnp.int32)
            present = jnp.sum(chosen) > 0
            x_start = jnp.sum(chosen * patch_corner[:, 0]) - 1
            y_start = jnp.sum(chosen * patch_corner[:, 1]) - 1

            def taken(fields, x_start=x_start, y_start=y_start):
                return refine(fields[0], fields[1], e_coef, x_start, y_start)

            efield, hfield = lax.cond(present, taken, lambda fields: fields, (efield, hfield))
        currents = accumulate(currents, efield, hfield, points, normals, omega, float(moment + 1))
    cell_x = lax.axis_index("gx") * block + points // (block * depth)
    cell_y = lax.axis_index("gy") * block + points // depth % block
    cell_z = points % depth
    positions = jnp.stack(
        [
            cell_x.astype(jnp.float32) + 0.5 - block * width_x / 2.0,
            cell_y.astype(jnp.float32) + 0.5 - block * width_y / 2.0,
            cell_z.astype(jnp.float32) + 0.5 - depth / 2.0,
        ]
    )
    scale = 1.0 / math.sqrt(points.shape[0] * width_x * width_y)
    far = lax.psum_scatter(
        project_blocks(angle_index, omega, currents, positions, scale),
        ("gx", "gy"),
        scatter_dimension=0,
        tiled=True,
    )
    return (efield, hfield, far)


def solution(mesh):
    placed = (
        P(None, "gx", "gy", None),
        P(None, "gx", "gy", None),
        P("gx", "gy", None),
        P(),
        P(),
        P(),
        P("gx", "gy", None),
        P("gx", "gy", None),
        P(),
    )
    return jax.shard_map(
        local,
        mesh=mesh,
        in_specs=placed,
        out_specs=(P(None, "gx", "gy", None), P(None, "gx", "gy", None), P(("gx", "gy"), None)),
        check_vma=False,
    )
```

profile of v0, /device:TPU:1, one launch (start us, length us, event | category | flops | bytes accessed | tf_op | source)
XLA Modules:
  0.0 1573.5 jit_solution(16924602910341132998)
XLA Ops:
  10.0 3.3 collective-permute-start
  39.3 3.2 collective-permute-start.2
  42.6 5.8 collective-permute-start.3
  52.5 36.3 %conditional.8 = ((f32[3,32,32,128]{3,2,1,0:T(8,128)S(1)}, f32[3,32,32,128]{3,2,1,0:T(8,128)S(1)})) conditional(s32[]{:T(128)} %convert_element_type.130, (f32[3,32,32,128]{3,2,1,0:T(8,128)S(1)}, f32[3,32,32,128]{3,2,1,0:T(8,128)S(1)}) %tuple.98, (s32[]{:T(128)}, s32[]{:T(128)}, f32[3,32,32,128]{3,2,1,0:T(8,128)S(1)}, f32[32,32,128]{2,1,0:T(8,128)}, ...), branch_computations={%region_7.8_spmd, %region_8.11_spmd} | conditional | flops 1715808640 | bytes 114906392 | solution.py:210
  64.0 3.4 fusion
  89.2 7.5 conditional.10
  96.7 8.5 conditional.11
  108.4 97.2 %collective-permute-done.5 = f32[2,1,32,128]{3,2,1,0:T(8,128)S(1)} collective-permute-done((f32[2,1,32,128]{3,2,1,0:T(8,128)S(1)}, f32[2,1,32,128]{3,2,1,0:T(8,128)S(1)}, u32[]{:S(2)}, u32[]{:S(2)}) %collective-permute-start.5) | collective-permute-done | bytes 32800 | tf_op jit(solution)/shard_map/ppermute | solution.py:21
  211.8 31.9 %copy.226 = f32[3,32,32,128]{0,3,2,1:T(8,128)} copy(f32[3,32,32,128]{3,2,1,0:T(8,128)S(1)} %get-tuple-element.325) | data formatting | bytes 3145728 | tf_op jit(solution)/shard_map/cond | solution.py:210
  245.9 31.9 %copy.249 = f32[3,32,32,128]{0,3,2,1:T(8,128)} copy(f32[3,32,32,128]{3,2,1,0:T(8,128)S(1)} %get-tuple-element.326) | data formatting | bytes 3145728
  290.3 3.6 collective-permute-start.6
  294.1 13.4 collective-permute-start.7
  312.1 34.0 %conditional.12 = ((f32[3,32,32,128]{3,2,1,0:T(8,128)}, f32[3,32,32,128]{3,2,1,0:T(8,128)S(1)})) conditional(s32[]{:T(128)} %convert_element_type.130, (f32[3,32,32,128]{3,2,1,0:T(8,128)}, f32[3,32,32,128]{3,2,1,0:T(8,128)S(1)}) %tuple.424, (s32[]{:T(128)}, s32[]{:T(128)}, f32[3,32,32,128]{3,2,1,0:T(8,128)}, f32[32,32,128]{2,1,0:T(8,128)}, ...), branch_computations={%region_29.30_spmd, %region_30.33_spmd} | conditional | flops 1715808640 | bytes 105075928 | solution.py:210
  322.3 3.4 fusion.148
  346.3 7.6 conditional.14
  354.0 9.0 conditional.15
  363.0 31.9 %copy.250 = f32[3,32,32,128]{0,3,2,1:T(8,128)} copy(f32[3,32,32,128]{3,2,1,0:T(8,128)S(1)} %get-tuple-element.328) | data formatting | bytes 3145728
  397.4 31.9 %copy.251 = f32[3,32,32,128]{0,3,2,1:T(8,128)} copy(f32[3,32,32,128]{3,2,1,0:T(8,128)S(1)} %copy-done.47) | data formatting | bytes 3145728
  432.3 402.2 %while.13 = (s32[]{:T(128)}, f32[8,512,48]{1,2,0:T(8,128)S(1)}, f32[4]{0:T(128)S(1)}, s32[8,512,2]{1,2,0:T(2,128)}, f32[3,256]{1,0:T(4,128)S(1)}, /*index=5*/f32[4,2,6,256]{3,2,1,0:T(8,128)S(1)}, s32[]{:T(128)}) while((s32[]{:T(128)}, f32[8,512,48]{1,2,0:T(8,128)S(1)}, f32[4]{0:T(128)S(1)}, s32[8,512,2]{1,2,0:T(2,128)}, ...), condition=%wide.region_46.48_spmd, body=%wide.region_45.47_spmd.sunk | while | flops 157867008 | bytes 9792693 | solution.py:168
  443.6 3.0 fusion.527
  493.9 3.0 fusion.527
  544.1 3.0 fusion.527
  644.6 3.0 fusion.527
  836.4 729.9 %reduce-scatter.2.cloned.1.call-done = f32[32,48]{1,0:T(8,128)} async-done(((f32[4096,48]{1,0:T(8,128)}), f32[32,48]{1,0:T(8,128)}) %reduce-scatter.2.cloned.1.call-update) | async-done | bytes 6160 | tf_op jit(solution)/shard_map/reduce_scatter | solution.py:223
  (500 shorter events, 513.5 us)
Async XLA Ops:
  7.2 1559.1 %reduce-scatter.2.cloned.1.call-start = ((), (), s32[]{:S(2)}) async-start(), calls=%async_computation.1 | async-start | bytes 2113536 | tf_op jit(solution)/shard_map/reduce_scatter | solution.py:223
  10.0 25.8 %collective-permute-start = (f32[2,32,1,128]{3,2,1,0:T(1,128)S(1)}, f32[2,32,1,128]{3,2,1,0:T(1,128)S(1)}, u32[]{:S(2)}, u32[]{:S(2)}) collective-permute-start(f32[2,32,1,128]{3,2,1,0:T(1,128)S(1)} %pad_maximum_fusion.24), channel_id=1, source_target_pairs={{1,0},{2,1},{3,2},{4,3},{5,4},{6,5},{7,6},{8,7},{9,8},{10,9},{11,1... | collective-permute-start | bytes 98312 | tf_op jit(solution)/shard_map/ppermute | solution.py:21
  13.4 20.7 %collective-permute-start.1 = (f32[2,1,32,128]{3,2,1,0:T(8,128)S(1)}, f32[2,1,32,128]{3,2,1,0:T(8,128)S(1)}, u32[]{:S(2)}, u32[]{:S(2)}) collective-permute-start(f32[2,1,32,128]{3,2,1,0:T(8,128)S(1)} %slice.1569), channel_id=1, source_target_pairs={{16,0},{32,16},{48,32},{64,48},{80,64},{96,80},{112,96},{17,1},{33... | collective-permute-start | bytes 98312 | tf_op jit(solution)/shard_map/ppermute | solution.py:21
  39.3 9.1 collective-permute-start.2
  42.6 6.8 collective-permute-start.3
  106.1 99.5 %copy-start.43 = (f32[3,32,32,128]{3,1,2,0:T(8,128)}, f32[3,32,32,128]{3,1,2,0:T(8,128)S(1)}, u32[]{:S(2)}) copy-start(f32[3,32,32,128]{3,1,2,0:T(8,128)S(1)} %copy.209) | copy-start | bytes 4718596
  106.2 104.7 %copy-start.56 = (f32[32,32,128]{2,1,0:T(8,128)}, f32[32,32,128]{2,1,0:T(8,128)S(1)}, u32[]{:S(2)}) copy-start(f32[32,32,128]{2,1,0:T(8,128)S(1)} %slice_bitcast_fusion.174) | copy-start | bytes 1572868
  106.2 99.4 %collective-permute-start.5 = (f32[2,1,32,128]{3,2,1,0:T(8,128)S(1)}, f32[2,1,32,128]{3,2,1,0:T(8,128)S(1)}, u32[]{:S(2)}, u32[]{:S(2)}) collective-permute-start(f32[2,1,32,128]{3,2,1,0:T(8,128)S(1)} %slice.1605), channel_id=1, source_target_pairs={{16,0},{32,16},{48,32},{64,48},{80,64},{96,80},{112,96},{17,1},{33... | collective-permute-start | bytes 98312 | tf_op jit(solution)/shard_map/ppermute | solution.py:21
  207.6 78.1 %collective-permute-start.4 = (f32[2,32,1,128]{3,2,1,0:T(1,128)S(1)}, f32[2,32,1,128]{3,2,1,0:T(1,128)S(1)}, u32[]{:S(2)}, u32[]{:S(2)}) collective-permute-start(f32[2,32,1,128]{3,2,1,0:T(1,128)S(1)} %pad_maximum_fusion.26), channel_id=1, source_target_pairs={{1,0},{2,1},{3,2},{4,3},{5,4},{6,5},{7,6},{8,7},{9,8},{10,9},{11,1... | collective-permute-start | bytes 98312 | tf_op jit(solution)/shard_map/ppermute | solution.py:21
  289.5 19.4 %copy-start.8 = (f32[3,32,32,128]{3,2,1,0:T(8,128)}, f32[3,32,32,128]{3,2,1,0:T(8,128)S(1)}, u32[]{:S(2)}) copy-start(f32[3,32,32,128]{3,2,1,0:T(8,128)S(1)} %fusion.375) | copy-start | bytes 4718596
  290.3 17.1 %collective-permute-start.6 = (f32[2,32,1,128]{3,1,2,0:T(8,128)S(1)}, f32[2,32,1,128]{3,1,2,0:T(8,128)S(1)}, u32[]{:S(2)}, u32[]{:S(2)}) collective-permute-start(f32[2,32,1,128]{3,1,2,0:T(8,128)S(1)} %pad_maximum_fusion.27), channel_id=1, source_target_pairs={{0,1},{1,2},{2,3},{3,4},{4,5},{5,6},{6,7},{7,8},{8,9},{9,10},{10,1... | collective-permute-start | bytes 98312 | tf_op jit(solution)/shard_map/ppermute | solution.py:21
  294.1 14.4 collective-permute-start.7
  363.0 31.9 %copy-start.10 = (f32[3,32,32,128]{3,2,1,0:T(8,128)}, f32[3,32,32,128]{3,2,1,0:T(8,128)S(1)}, u32[]{:S(2)}) copy-start(f32[3,32,32,128]{3,2,1,0:T(8,128)S(1)} %get-tuple-element.328) | copy-start | bytes 4718596
  363.0 34.3 %copy-start.47 = (f32[3,32,32,128]{3,2,1,0:T(8,128)S(1)}, f32[3,32,32,128]{3,2,1,0:T(8,128)}, u32[]{:S(2)}) copy-start(f32[3,32,32,128]{3,2,1,0:T(8,128)} %get-tuple-element.327) | copy-start | bytes 4718596
  397.3 34.4 %copy-start.112 = (f32[256,3]{0,1:T(4,128)S(1)}, f32[256,3]{0,1:T(4,128)}, u32[]{:S(2)}) copy-start(f32[256,3]{0,1:T(4,128)} %copy.227) | copy-start | bytes 9220
  397.4 34.4 %copy-start.121 = (pred[256]{0:T(512)(128)(4,1)S(1)}, pred[256]{0:T(512)(128)(4,1)}, u32[]{:S(2)}) copy-start(pred[256]{0:T(512)(128)(4,1)} %compare_and_fusion.8) | copy-start | bytes 772
  397.4 34.5 %copy-start.114 = (s32[1,1,256]{2,1,0:T(1,128)S(1)}, s32[1,1,256]{2,1,0:T(1,128)}, u32[]{:S(2)}) copy-start(s32[1,1,256]{2,1,0:T(1,128)} %param.35) | copy-start | bytes 3076
  397.4 34.5 %copy-start.120 = (s32[1,1,256]{2,1,0:T(1,128)S(1)}, s32[1,1,256]{2,1,0:T(1,128)}, u32[]{:S(2)}) copy-start(s32[1,1,256]{2,1,0:T(1,128)} %param.36) | copy-start | bytes 3076
  397.4 34.6 %copy-start.117 = (f32[4]{0:T(128)S(1)}, f32[4]{0:T(128)}, u32[]{:S(2)}) copy-start(f32[4]{0:T(128)} %get-tuple-element.733) | copy-start | bytes 52
  397.4 34.6 %copy-start.118 = (f32[4]{0:T(128)S(1)}, f32[4]{0:T(128)}, u32[]{:S(2)}) copy-start(f32[4]{0:T(128)} %get-tuple-element.734) | copy-start | bytes 52
  397.4 34.7 %copy-start.115 = (f32[4]{0:T(128)S(1)}, f32[4]{0:T(128)}, u32[]{:S(2)}) copy-start(f32[4]{0:T(128)} %get-tuple-element.735) | copy-start | bytes 52
  397.4 34.7 %copy-start.116 = (f32[4]{0:T(128)S(1)}, f32[4]{0:T(128)}, u32[]{:S(2)}) copy-start(f32[4]{0:T(128)} %get-tuple-element.736) | copy-start | bytes 52
  397.4 34.8 %copy-start.109 = (f32[8,512,48]{1,2,0:T(8,128)S(1)}, f32[8,512,48]{1,2,0:T(8,128)}, u32[]{:S(2)}) copy-start(f32[8,512,48]{1,2,0:T(8,128)} %custom-call.8) | copy-start | bytes 2359300
  397.4 34.8 %copy-start.111 = (f32[4]{0:T(128)S(1)}, f32[4]{0:T(128)}, u32[]{:S(2)}) copy-start(f32[4]{0:T(128)} %param.32) | copy-start | bytes 52
  (42 other events, 83.4 us)
Sparse Core Ops, SparseCore 0:
  836.5 729.7 reduce-scatter.1
where the time goes:
time: 1590 us; the launch traced here: 1570 us
  waiting for transfers between devices  829 us (52%)
  matrix products  401 us (25%)
  local copies, waits for them, and re-layouts  215 us (14%)
  other arithmetic  36 us (2%)
  loops' own time  34.8 us (2%)
  starting transfers between devices  34.4 us (2%)
  between operations  22.9 us (1%)
    reduce_scatter x1, waiting for transfers between devices, local(): lax.psum_scatter(project_blocks(angle_index, omega, currents, positions,...  730 us
    unnamed x81, local copies, waits for them, and re-layouts  108 us
    ppermute x8, waiting for transfers between devices, passed_along(): return lax.ppermute(block, axis, route)  98.8 us
    dot_general x32, matrix products, project(): jnp.dot(sine, imag_cur, precision=hp)  95.6 us
    dot_general x32, matrix products, project(): jnp.dot(sine, real_cur, precision=hp)  95.4 us
    dot_general x32, matrix products, project(): jnp.dot(cosine, imag_cur, precision=hp)  95.1 us
    dot_general x32, matrix products, project(): jnp.dot(cosine, real_cur, precision=hp)  95.1 us
    ppermute x8, starting transfers between devices, passed_along(): return lax.ppermute(block, axis, route)  34.3 us
  transfers between devices with their start and end apart: 9, of which 4 were waited for; matrix products, arithmetic and copies ran while one was open for 6% of the time, Pallas kernels for 0%

commit v1 on v0

v1 whole, which is shorter than its diff:
```python
import math

import jax
import jax.numpy as jnp
import numpy as np
from jax import lax
from jax.experimental import pallas as pl
from jax.experimental.pallas import tpu as pltpu
from jax.sharding import PartitionSpec as P

PB = 8
SLOTS = 4
NTH = 128
NPH = 256
CB = 32
CZ = 128
ROWS = CB * CB
SPB = 256
FREQ = 4
GX = 8
GY = 16
ANG = 4096
QN = ANG // GX
QF = QN * FREQ
OWN = ANG // (GX * GY)
MESH = pl.DeviceIdType.MESH
F32 = jnp.float32
BF16 = jnp.bfloat16


def lanes_of(shape):
    return lax.broadcasted_iota(jnp.int32, shape, 1)


def rows_of(shape):
    return lax.broadcasted_iota(jnp.int32, shape, 0)


def z_next(v):
    return jnp.where(lanes_of(v.shape) == CZ - 1, 0.0, pltpu.roll(v, CZ - 1, 1))


def z_prev(v):
    return jnp.where(lanes_of(v.shape) == 0, 0.0, pltpu.roll(v, 1, 1))


def y_next(v, edge):
    n = v.shape[0]
    return jnp.where(rows_of(v.shape) == n - 1, edge, pltpu.roll(v, n - 1, 0))


def y_prev(v, edge):
    return jnp.where(rows_of(v.shape) == 0, edge, pltpu.roll(v, 1, 0))


def prepare(es, hs, out):
    out[0] = es[1, 0:CB]
    out[1] = es[2, 0:CB]
    last = (CB - 1) * CB
    ex, ey, ez = [es[k, last : last + CB] for k in range(3)]
    hy, hz = [hs[k, last + CB : last + 2 * CB] for k in (1, 2)]
    out[2] = hy - 0.5 * (z_next(ex) - ex + ez)
    out[3] = hz + 0.5 * (ey + y_next(ex, 0.0) - ex)
    out[8, 8:16] = ey[CB - 8 : CB] * 0.0 + es[1, CB - 1 : CB]
    out[8, 0:8] = ex[0:1] + jnp.zeros((8, CZ), F32)
    out[8, 16:32] = jnp.zeros((16, CZ), F32)
    out[4] = es[0, pl.ds(0, CB, stride=CB)]
    out[5] = es[2, pl.ds(0, CB, stride=CB)]
    ex, ey, ez = [es[k, pl.ds(CB - 1, CB, stride=CB)] for k in range(3)]
    hx, hz = [hs[k, pl.ds(2 * CB - 1, CB, stride=CB)] for k in (0, 2)]
    out[6] = hx + 0.5 * (ez + z_next(ey) - ey)
    out[7] = hz - 0.5 * (y_next(ey, 0.0) - ey + ex)


def place_halo(es, hs, halo, ye, yh):
    gx = lax.axis_index("gx")
    gy = lax.axis_index("gy")
    x_low = (gx > 0).astype(F32)
    x_high = (gx < GX - 1).astype(F32)
    y_low = (gy > 0).astype(F32)
    y_high = (gy < GY - 1).astype(F32)
    last_row = rows_of((CB, CZ)) == CB - 1
    es[1, ROWS : ROWS + CB] = halo[0] * x_high
    es[2, ROWS : ROWS + CB] = halo[1] * x_high
    ye[0] = halo[4] * y_high
    ye[1] = halo[5] * y_high
    corner = jnp.where(last_row, halo[8, 0:1] * (0.5 * y_high), 0.0)
    hs[1, 0:CB] = x_low * (halo[2] + 0.5 * es[2, 0:CB])
    hs[2, 0:CB] = x_low * (halo[3] - 0.5 * es[1, 0:CB] + corner)
    corner = jnp.where(last_row, halo[8, 8:9] * (0.5 * x_high), 0.0)
    yh[0] = y_low * (halo[6] - 0.5 * es[2, pl.ds(0, CB, stride=CB)])
    yh[1] = y_low * (halo[7] + 0.5 * es[0, pl.ds(0, CB, stride=CB)] - corner)


def advance(es, hs, cs, ye, yh):
    def slab(x, carry):
        r = pl.multiple_of(x * CB, CB)
        here = pl.ds(r, CB)
        after = pl.ds(pl.multiple_of(r + CB, CB), CB)
        ex, ey, ez = [es[k, here] for k in range(3)]
        ey1, ez1 = es[1, after], es[2, after]
        hx, hy, hz = [hs[k, after] for k in range(3)]
        hy0, hz0 = hs[1, here], hs[2, here]
        row = pl.ds(x, 1)
        hx = hx - 0.5 * (y_next(ez, ye[1, row]) - ez - z_next(ey) + ey)
        hy = hy - 0.5 * (z_next(ex) - ex - ez1 + ez)
        hz = hz - 0.5 * (ey1 - ey - y_next(ex, ye[0, row]) + ex)
        c = cs[here]
        ex = ex + c * (hz - y_prev(hz, yh[1, row]) - hy + z_prev(hy))
        ey = ey + c * (hx - z_prev(hx) - hz + hz0)
        ez = ez + c * (hy - hy0 - hx + y_prev(hx, yh[0, row]))
        for k, v in enumerate((hx, hy, hz)):
            hs[k, after] = v
        for k, v in enumerate((ex, ey, ez)):
            es[k, here] = v
        return carry

    lax.fori_loop(0, CB, slab, 0)


def neighbours():
    gx = lax.axis_index("gx")
    gy = lax.axis_index("gy")
    xn, xp = lax.rem(gx + 1, GX), lax.rem(gx + GX - 1, GX)
    yn, yp = lax.rem(gy + 1, GY), lax.rem(gy + GY - 1, GY)
    return [(xp, gy), (xn, gy), (gx, yp), (gx, yn), (xn, yp), (xp, yn)]


def pieces(ref, n):
    if n < 4:
        return ref.at[pl.ds(2 * n, 2)]
    return ref.at[8, pl.ds(8 * (n - 4), 8)]


def first_kernel(e_in, h_in, c_in, e_out, h_out, halo2, es, hs, cs, ye, yh, sent, halo1, local_sem, send_sem, recv_sem):
    loads = [
        pltpu.make_async_copy(e_in, es.at[:, pl.ds(0, ROWS)], local_sem.at[0]),
        pltpu.make_async_copy(h_in, hs.at[:, pl.ds(CB, ROWS)], local_sem.at[1]),
        pltpu.make_async_copy(c_in, cs, local_sem.at[2]),
    ]
    for copy in loads:
        copy.start()
    barrier = pltpu.get_barrier_semaphore()
    for device in neighbours():
        pl.semaphore_signal(barrier, inc=1, device_id=device, device_id_type=MESH)
    loads[0].wait()
    loads[1].wait()

    def exchange(number, halo):
        copies = []
        for n, device in enumerate(neighbours()):
            copy = pltpu.make_async_remote_copy(
                src_ref=pieces(sent.at[number], n),
                dst_ref=pieces(halo, n),
                send_sem=send_sem.at[number, n],
                recv_sem=recv_sem.at[number, n],
                device_id=device,
                device_id_type=MESH,
            )
            copy.start()
            copies.append(copy)
        return copies

    prepare(es, hs, sent.at[0])
    pl.semaphore_wait(barrier, 6)
    copies = exchange(0, halo1)
    loads[2].wait()
    for copy in copies:
        copy.wait()
    place_halo(es, hs, halo1, ye, yh)
    advance(es, hs, cs, ye, yh)
    prepare(es, hs, sent.at[1])
    copies = exchange(1, halo2)
    stores = [
        pltpu.make_async_copy(es.at[:, pl.ds(0, ROWS)], e_out, local_sem.at[0]),
        pltpu.make_async_copy(hs.at[:, pl.ds(CB, ROWS)], h_out, local_sem.at[1]),
    ]
    for copy in stores:
        copy.start()
    for copy in copies + stores:
        copy.wait()


def patch(es, hs, cs, x0, y0):
    first = rows_of((PB, CZ)) == 0
    final = rows_of((PB, CZ)) == PB - 1

    def e_at(k, i, j):
        return es[k, pl.ds((x0 + i) * CB + y0 + j, PB)]

    def h_at(k, i, j):
        return hs[k, pl.ds((x0 + i + 1) * CB + y0 + j, PB)]

    def up(v, edge):
        return jnp.where(final, edge, pltpu.roll(v, PB - 1, 0))

    def down(v, edge):
        return jnp.where(first, edge, pltpu.roll(v, 1, 0))

    class Cell:
        pass

    def averages(name, o, e, c, u1, u0, wu, v1, v0, wv, pa, pb):
        vm = 0.5 * (v0 + v1)
        um = 0.5 * (u0 + u1)
        qu = 0.25 * wu
        qv = 0.25 * wv
        base_a = e - c * (vm + qv)
        base_b = e + c * (um - qu)
        setattr(o, name + pa + "1", base_a + c * u1)
        setattr(o, name + pa + "0", base_a + c * (u0 - 0.5 * wu))
        setattr(o, name + pb + "1", base_b - c * v1)
        setattr(o, name + pb + "0", base_b - c * (v0 + 0.5 * wv))
        setattr(o, name + "s" + pa + "0", e + c * (u0 - wu - vm - 0.5 * wv))
        setattr(o, name + "s" + pb + "0", e + c * (um - 0.5 * wu - v0 - wv))

    def stage_one(i):
        o = Cell()
        ex, ey, ez = [e_at(k, i, 0) for k in range(3)]
        exu, ezu = e_at(0, i, 1), e_at(2, i, 1)
        exd, eyd, ezd = [e_at(k, i, -1) for k in range(3)]
        exf, eyf, ezf = [e_at(k, i + 1, 0) for k in range(3)]
        eyb, ezb = e_at(1, i - 1, 0), e_at(2, i - 1, 0)
        exbu, exb = e_at(0, i - 1, 1), e_at(0, i - 1, 0)
        eyfd = e_at(1, i + 1, -1)
        hx, hy, hz = [h_at(k, i, 0) for k in range(3)]
        hxd, hzd = h_at(0, i, -1), h_at(2, i, -1)
        hyb, hzb = h_at(1, i - 1, 0), h_at(2, i - 1, 0)
        c = cs[pl.ds((x0 + i) * CB + y0, PB)]
        dyex, dyez = exu - ex, ezu - ez
        dxey, dxez = eyf - ey, ezf - ez
        dzex, dzey = z_next(ex) - ex, z_next(ey) - ey
        dyexb = exbu - exb
        dxeyd = eyfd - eyd
        szex, szey = z_prev(dzex), z_prev(dzey)
        averages(
            "x", o, ex, c,
            0.5 * dyex, hz - hzd - 0.5 * (ex - exd), 0.5 * (dxey - dxeyd),
            -0.5 * dzex, hy - z_prev(hy) + 0.5 * szex, 0.5 * (dxez - z_prev(dxez)),
            "y", "z",
        )
        averages(
            "y", o, ey, c,
            0.5 * dzey, hx - z_prev(hx) - 0.5 * szey, 0.5 * (dyez - z_prev(dyez)),
            -0.5 * dxey, hz - hzb + 0.5 * (ey - eyb), 0.5 * (dyex - dyexb),
            "z", "x",
        )
        dzexb = z_next(exb) - exb
        dzeyd = z_next(eyd) - eyd
        averages(
            "z", o, ez, c,
            0.5 * dxez, hy - hyb - 0.5 * (ez - ezb), 0.5 * (dzex - dzexb),
            -0.5 * dyez, hx - hxd + 0.5 * (ez - ezd), 0.5 * (dzey - dzeyd),
            "x", "y",
        )
        o.c = c
        o.h = (hx, hy, hz)
        o.d = (dyez, dzey, dzex, dxez, dxey, dyex)
        o.down = (exd, eyd, ezd, eyfd, hxd, hzd, dzeyd)
        o.up = (exu, ezu, e_at(1, i, 1))
        return o

    def ring_ahead(i):
        o = Cell()
        ey, ez = e_at(1, i, 0), e_at(2, i, 0)
        o.yx0 = o.ysx0 = ey
        o.zx0 = o.zsx0 = ez
        return o

    def ring_behind(o):
        ex, ey, ez = [e_at(k, -1, 0) for k in range(3)]
        h2zx = h_at(2, -1, 0) - 0.5 * (o.yx0 - ey) + 0.25 * (e_at(0, -1, 1) - ex)
        h2yx = h_at(1, -1, 0) - 0.25 * (z_next(ex) - ex) + 0.5 * (o.zx0 - ez)
        return h2zx, h2yx

    def stage_two(o, n, behind):
        hx, hy, hz = o.h
        dyez, dzey, dzex, dxez, dxey, dyex = o.d
        exd, eyd, ezd, eyfd, hxd, hzd, dzeyd = o.down
        exu, ezu, eyu = o.up
        h2zx_b, h2yx_b = behind
        xy0u = up(o.xy0, exu)
        zy0u = up(o.zy0, ezu)
        h2zy = hz - 0.25 * dxey + 0.5 * dyex - 0.25 * (n.ysx0 - o.ysx0) + 0.5 * (xy0u - o.xy1)
        h2zx = hz - 0.5 * dxey + 0.25 * dyex - 0.5 * (n.yx0 - o.yx1) + 0.25 * (up(o.xsy0, exu) - o.xsy0)
        h2xz = hx - 0.25 * dyez + 0.5 * dzey - 0.25 * (up(o.zsy0, ezu) - o.zsy0) + 0.5 * (z_next(o.yz0) - o.yz1)
        h2xy = hx - 0.5 * dyez + 0.25 * dzey - 0.5 * (zy0u - o.zy1) + 0.25 * (z_next(o.ysz0) - o.ysz0)
        h2yx = hy - 0.25 * dzex + 0.5 * dxez - 0.25 * (z_next(o.xsz0) - o.xsz0) + 0.5 * (n.zx0 - o.zx1)
        h2yz = hy - 0.5 * dzex + 0.25 * dxez - 0.5 * (z_next(o.xz0) - o.xz1) + 0.25 * (n.zsx0 - o.zsx0)
        h2zy_d = down(h2zy, hzd - 0.25 * (eyfd - eyd) + 0.5 * (o.xy0 - exd))
        h2xy_d = down(h2xy, hxd - 0.5 * (o.zy0 - ezd) + 0.25 * dzeyd)
        half = 0.5 * o.c
        ex = 0.5 * (o.xy0 + o.xy1) + half * (h2zy - h2zy_d - h2yz + z_prev(h2yz))
        ey = 0.5 * (o.yz0 + o.yz1) + half * (h2xz - z_prev(h2xz) - h2zx + h2zx_b)
        ez = 0.5 * (o.zx0 + o.zx1) + half * (h2yx - h2yx_b - h2xy + h2xy_d)
        hx = hx - 0.25 * (dyez - dzey + zy0u - o.zy0 - z_next(o.yz0) + o.yz0)
        hy = hy - 0.25 * (dzex - dxez + z_next(o.xz0) - o.xz0 - n.zx0 + o.zx0)
        hz = hz - 0.25 * (dxey - dyex + n.yx0 - o.yx0 - xy0u + o.xy0)
        return (ex, ey, ez), (hx, hy, hz), (h2zx, h2yx)

    now = stage_one(0)
    behind = ring_behind(now)
    for i in range(PB):
        later = stage_one(i + 1) if i < PB - 1 else ring_ahead(i + 1)
        e_new, h_new, behind = stage_two(now, later, behind)
        pending = (i, e_new, h_new)
        if i > 0:
            write(es, hs, x0, y0, previous)
        previous = pending
        now = later
    write(es, hs, x0, y0, previous)


def write(es, hs, x0, y0, item):
    i, e_new, h_new = item
    for k in range(3):
        es[k, pl.ds((x0 + i) * CB + y0, PB)] = e_new[k]
        hs[k, pl.ds((x0 + i + 1) * CB + y0, PB)] = h_new[k]


def second_kernel(owner, corner, points, faces, place, halo, e_in, h_in, c_in, e_out, h_out, sampled, es, hs, cs, ye, yh, taken, slot_x, slot_y, count, sem):
    loads = [
        pltpu.make_async_copy(e_in, es.at[:, pl.ds(0, ROWS)], sem.at[0]),
        pltpu.make_async_copy(h_in, hs.at[:, pl.ds(CB, ROWS)], sem.at[1]),
        pltpu.make_async_copy(c_in, cs, sem.at[2]),
    ]
    for copy in loads:
        copy.start()
    me = lax.axis_index("gx") * GY + lax.axis_index("gy")

    def look(n, found):
        slot_x[found] = corner[2 * n]
        slot_y[found] = corner[2 * n + 1]
        return jnp.minimum(found + (owner[n] == me).astype(jnp.int32), SLOTS)

    count[0] = lax.fori_loop(0, GX * GY, look, 0, unroll=8)
    for copy in loads:
        copy.wait()
    lane = lanes_of((1, CZ))

    def patches():
        def one(n, carry):
            patch(es, hs, cs, slot_x[n], slot_y[n])
            return carry

        lax.fori_loop(0, count[0], one, 0)

    def sample():
        def one(n, carry):
            cell = jnp.maximum(points[n], 0)
            row = cell // CZ
            mask = lane == cell % CZ
            k = faces[n] // 2
            k1 = jnp.where(k == 2, 0, k + 1)
            k2 = jnp.where(k == 0, 2, k - 1)
            taken[pl.ds(n + 0 * SPB, 1)] = jnp.where(mask, hs[k1, pl.ds(row + CB, 1)], 0.0)
            taken[pl.ds(n + 1 * SPB, 1)] = jnp.where(mask, hs[k2, pl.ds(row + CB, 1)], 0.0)
            taken[pl.ds(n + 2 * SPB, 1)] = jnp.where(mask, es[k1, pl.ds(row, 1)], 0.0)
            taken[pl.ds(n + 3 * SPB, 1)] = jnp.where(mask, es[k2, pl.ds(row, 1)], 0.0)
            return carry

        lax.fori_loop(0, SPB, one, 0, unroll=8)
        return lax.dot_general(
            jnp.ones((8, CZ), F32), taken[...], (((1,), (1,)), ((), ())),
            precision=lax.Precision.HIGHEST, preferred_element_type=F32,
        )

    slots = place[0:1]
    face = place[1:2]
    sign = jnp.where(slots >= 0, (2 * (face % 2) - 1).astype(F32), 0.0)
    for moment in range(2):
        if moment:
            place_halo(es, hs, halo, ye, yh)
            advance(es, hs, cs, ye, yh)
        patches()
        if moment:
            stores = [
                pltpu.make_async_copy(es.at[:, pl.ds(0, ROWS)], e_out, sem.at[0]),
                pltpu.make_async_copy(hs.at[:, pl.ds(CB, ROWS)], h_out, sem.at[1]),
            ]
            for copy in stores:
                copy.start()
        got = sample()
        got = [got[0:1, j * SPB : (j + 1) * SPB] for j in range(4)]
        sampled[4 * moment : 4 * moment + 1] = -sign * got[1]
        sampled[4 * moment + 1 : 4 * moment + 2] = sign * got[0]
        sampled[4 * moment + 2 : 4 * moment + 3] = sign * got[3]
        sampled[4 * moment + 3 : 4 * moment + 4] = -sign * got[2]
    cell = jnp.maximum(slots, 0)
    sampled[8:9] = (cell // (CB * CZ)).astype(F32)
    sampled[9:10] = (cell // CZ % CB).astype(F32)
    sampled[10:11] = (cell % CZ).astype(F32)
    sampled[11:12] = jnp.where(slots >= 0, face, 6).astype(F32)
    sampled[12:16] = jnp.zeros((4, SPB), F32)
    for copy in stores:
        copy.wait()


def fitted(function, degrees, points=4001):
    r = np.cos(np.linspace(0.0, np.pi, points)) * 0.5
    basis = np.stack([r**d for d in degrees], axis=1)
    return [float(v) for v in np.linalg.lstsq(basis, function(np.pi * r) * math.sqrt(2.0), rcond=None)[0]]


SIN = fitted(np.sin, (1, 3, 5, 7, 9))
COS = fitted(np.cos, (0, 2, 4, 6, 8))


def turn(t):
    r = t - jnp.round(t)
    r2 = r * r
    s = r * (SIN[0] + r2 * (SIN[1] + r2 * (SIN[2] + r2 * (SIN[3] + r2 * SIN[4]))))
    c = COS[0] + r2 * (COS[1] + r2 * (COS[2] + r2 * (COS[3] + r2 * COS[4])))
    return 1.0 - s * s, s * c


def split(v):
    high = v.astype(BF16)
    return high, (v - high.astype(F32)).astype(BF16)


def dot(a, b):
    return jnp.dot(a, b, preferred_element_type=F32)


def dot_t(a, b):
    return lax.dot_general(a, b, (((1,), (1,)), ((), ())), preferred_element_type=F32)


XF = 128
ZF = 64
YF_ROWS = 96
CHUNK = 256
X_FACE = 111
Z_FACE = 47


def third_kernel(omega, sampled, angles, far, got, gathered, kdir, ta, tc, tb, tcf, hot, spread_hi, spread_lo, lhs1, lhs2, lhsz, big, acc, rows48, send_buf, recv_buf, send1, recv1, send2, recv2):
    gx = lax.axis_index("gx")
    gy = lax.axis_index("gy")
    barrier = pltpu.get_barrier_semaphore()
    for d in range(1, GX):
        pl.semaphore_signal(barrier, inc=1, device_id=(lax.rem(gx + d, GX), gy), device_id_type=MESH)
    for d in range(1, GY):
        pl.semaphore_signal(barrier, inc=1, device_id=(gx, lax.rem(gy + d, GY)), device_id_type=MESH)
    pl.semaphore_wait(barrier, GX + GY - 2)
    first = []
    for d in range(1, GX):
        copy = pltpu.make_async_remote_copy(
            src_ref=sampled,
            dst_ref=gathered.at[GX - d],
            send_sem=send1.at[d],
            recv_sem=recv1.at[GX - d],
            device_id=(lax.rem(gx + d, GX), gy),
            device_id_type=MESH,
        )
        copy.start()
        first.append(copy)

    index = angles[...].astype(F32)
    theta = math.pi * (index[0:1] + 0.5) / NTH
    phi = 2.0 * math.pi * (index[1:2] + 0.5) / NPH
    st, ct = jnp.sin(theta), jnp.cos(theta)
    sp, cp = jnp.sin(phi), jnp.cos(phi)
    for f in range(FREQ):
        w = omega[f] * (1.0 / (2.0 * math.pi))
        kdir[0:1, f * QN : (f + 1) * QN] = st * cp * w
        kdir[1:2, f * QN : (f + 1) * QN] = st * sp * w
        kdir[2:3, f * QN : (f + 1) * QN] = ct * w

    y_start = (gy * CB).astype(F32) + (0.5 - CB * GY / 2.0)

    def tables(n, carry):
        lanes = pl.ds(pl.multiple_of(n * CHUNK, CHUNK), CHUNK)
        kx, ky, kz = kdir[0:1, lanes], kdir[1:2, lanes], kdir[2:3, lanes]
        for j in range(0, XF, 16):
            at = rows_of((16, CHUNK)).astype(F32) + (j + 0.5)
            for k, v in enumerate(turn(at * kx)):
                high, low = split(v)
                ta[k, j : j + 16, lanes] = high
                ta[k, XF + j : XF + j + 16, lanes] = low
        for j in range(0, ZF, 16):
            at = rows_of((16, CHUNK)).astype(F32) + (j + 0.5)
            for k, v in enumerate(turn(at * kz)):
                high, low = split(v)
                tc[k, j : j + 16, lanes] = high
                tc[k, ZF + j : ZF + j + 16, lanes] = low
                tc[k, 2 * ZF + j : 2 * ZF + j + 16, lanes] = high
                tc[k, 3 * ZF + j : 3 * ZF + j + 16, lanes] = jnp.zeros((16, CHUNK), BF16)
                tcf[k, j : j + 16, lanes] = v
        for j in range(0, CB, 16):
            at = rows_of((16, CHUNK)).astype(F32) + (y_start + j)
            for k, v in enumerate(turn(at * ky)):
                tb[k, j : j + 16, lanes] = v
        at = jnp.full((8, CHUNK), X_FACE + 0.5, F32)
        for k, v in enumerate(turn(at * kx)):
            tb[k, CB : CB + 8, lanes] = v
        return carry

    lax.fori_loop(0, QF // CHUNK, tables, 0)
    gathered[0] = sampled[...]
    for copy in first:
        copy.wait()

    for b in range(GX):
        lanes = slice(b * SPB, (b + 1) * SPB)
        got[0:16, lanes] = gathered[b]
        block = lax.rem(gx + b, GX)
        x = gathered[b, 8:9] + (block * CB).astype(F32)
        z = gathered[b, 10:11]
        got[12:13, lanes] = jnp.where(x < 128.0, 127.0 - x, x - 128.0)
        got[13:14, lanes] = jnp.where(x < 128.0, -1.0, 1.0)
        got[14:15, lanes] = jnp.where(z < 64.0, 63.0 - z, z - 64.0)
        got[15:16, lanes] = jnp.where(z < 64.0, -1.0, 1.0)

    slots = GX * SPB

    def one_hot(place_row, sign_row, count):
        for b in range(GX):
            lanes = slice(b * SPB, (b + 1) * SPB)
            where_at = got[place_row : place_row + 1, lanes]
            sign = got[sign_row : sign_row + 1, lanes]
            for j in range(0, count, 16):
                at = rows_of((16, SPB)).astype(F32) + float(j)
                same = at == where_at
                hot[j : j + 16, lanes] = jnp.where(same, 1.0, 0.0).astype(BF16)
                hot[count + j : count + j + 16, lanes] = jnp.where(same, sign, 0.0).astype(BF16)

    def spread(low_face, high_face):
        for b in range(GX):
            lanes = slice(b * SPB, (b + 1) * SPB)
            cols = got[0:8, lanes]
            face = got[11:12, lanes]
            v = jnp.concatenate([jnp.where(face == low_face, cols, 0.0), jnp.where(face == high_face, cols, 0.0)], axis=0)
            high = v.astype(BF16).astype(F32)
            low = v - high
            ys = got[9:10, lanes]

            def one(y, carry):
                same = ys == y.astype(F32)
                at = pl.ds(pl.multiple_of(y * 16, 16), 16)
                spread_hi[at, lanes] = jnp.where(same, high, 0.0).astype(BF16)
                spread_lo[at, lanes] = jnp.where(same, low, 0.0).astype(BF16)
                return carry

            lax.fori_loop(0, CB, one, 0, unroll=4)

    def spread_y():
        for b in range(GX):
            lanes = slice(b * SPB, (b + 1) * SPB)
            face = got[11:12, lanes]
            v = jnp.where((face == 2.0) | (face == 3.0), got[0:8, lanes], 0.0)
            v = jnp.concatenate([v, v], axis=0)
            high = v.astype(BF16).astype(F32)
            low = v - high
            zs = got[10:11, lanes]
            second = (rows_of((16, SPB)) // 8).astype(F32)

            def one(o, carry):
                same = zs == second + (2 * o + 16).astype(F32)
                at = pl.ds(pl.multiple_of(o * 16, 16), 16)
                spread_hi[at, lanes] = jnp.where(same, high, 0.0).astype(BF16)
                spread_lo[at, lanes] = jnp.where(same, low, 0.0).astype(BF16)
                return carry

            lax.fori_loop(0, YF_ROWS // 2, one, 0, unroll=4)

    def dense(count):
        for m in range(0, count, CHUNK):
            d = dot_t(spread_hi[m : m + CHUNK], hot[...]) + dot_t(spread_lo[m : m + CHUNK], hot[...])
            for k in range(2):
                high, low = split(d[:, k * XF : (k + 1) * XF])
                lhs1[k, m : m + CHUNK, 0:XF] = high
                lhs1[k, m : m + CHUNK, XF : 2 * XF] = high
                lhs2[k, m : m + CHUNK] = low

    one_hot(12, 13, XF)
    spread(4.0, 5.0)
    dense(CB * 16)

    def outer_y(n, base):
        lanes = pl.ds(pl.multiple_of(n * CHUNK, CHUNK), CHUNK)

        def one(y, total):
            re, im = total
            at = pl.ds(pl.multiple_of(y * 16, 16), 16)
            g_re, g_im = big[0, at], big[1, at]
            bc, bs = tb[0, pl.ds(y, 1), lanes], tb[1, pl.ds(y, 1), lanes]
            return re + (bc * g_re - bs * g_im), im + (bc * g_im + bs * g_re)

        zero = jnp.zeros((16, CHUNK), F32)
        re, im = lax.fori_loop(0, CB, one, (zero, zero), unroll=4)
        acc[base, 0, :, lanes] = re
        acc[base, 1, :, lanes] = im

    def across_z(n, carry):
        lanes = pl.ds(pl.multiple_of(n * CHUNK, CHUNK), CHUNK)
        for k in range(2):
            table = ta[k, :, lanes]
            big[k, 0 : CB * 16] = dot(lhs1[k, 0 : CB * 16], table) + dot(lhs2[k, 0 : CB * 16], table[0:XF])
        outer_y(n, 0)
        return carry

    lax.fori_loop(0, QF // CHUNK, across_z, 0)
    edge = (gy == 0) | (gy == GY - 1)

    @pl.when(jnp.logical_not(edge))
    def _():
        acc[2] = jnp.zeros((2, 16, QF), F32)

    @pl.when(edge)
    def _():
        spread_y()
        dense(YF_ROWS * 8)

        def across_y(n, carry):
            lanes = pl.ds(pl.multiple_of(n * CHUNK, CHUNK), CHUNK)
            for k in range(2):
                table = ta[k, :, lanes]
                big[k] = dot(lhs1[k], table) + dot(lhs2[k], table[0:XF])

            def one(o, total):
                re, im = total
                below = pl.ds(pl.multiple_of((Z_FACE - o) * 8, 8), 8)
                above = pl.ds(pl.multiple_of((Z_FACE + 1 + o) * 8, 8), 8)
                cc, cs = tcf[0, pl.ds(o, 1), lanes], tcf[1, pl.ds(o, 1), lanes]
                a_re, a_im, b_re, b_im = big[0, above], big[1, above], big[0, below], big[1, below]
                re = re + (cc * (a_re + b_re) - cs * (a_im - b_im))
                im = im + (cc * (a_im + b_im) + cs * (a_re - b_re))
                return re, im

            zero = jnp.zeros((8, CHUNK), F32)
            re, im = lax.fori_loop(0, YF_ROWS // 2, one, (zero, zero), unroll=4)
            acc[2, 0, 0:8, lanes] = re
            acc[2, 1, 0:8, lanes] = im
            return carry

        lax.fori_loop(0, QF // CHUNK, across_y, 0)

    one_hot(14, 15, ZF)
    spread(0.0, 1.0)
    for m in range(0, CB * 16, CHUNK):
        d = dot_t(spread_hi[m : m + CHUNK], hot[0 : 2 * ZF]) + dot_t(spread_lo[m : m + CHUNK], hot[0 : 2 * ZF])
        for k in range(2):
            high, low = split(d[:, k * ZF : (k + 1) * ZF])
            lhsz[k, m : m + CHUNK] = jnp.concatenate([high, high, low, jnp.zeros_like(low)], axis=1)

    def across_x(n, carry):
        lanes = pl.ds(pl.multiple_of(n * CHUNK, CHUNK), CHUNK)
        for k in range(2):
            big[k, 0 : CB * 16] = dot(lhsz[k], tc[k, :, lanes])
        outer_y(n, 1)
        return carry

    lax.fori_loop(0, QF // CHUNK, across_x, 0)

    scale = 1.0 / math.sqrt(GX * GY * SPB)
    y_face = jnp.where(gy == 0, 16, 15)
    moment = 1.0 + (rows_of((8, 1)) // 4).astype(F32)
    for f in range(FREQ):
        lanes = slice(f * QN, (f + 1) * QN)
        mc, ms = turn(omega[f] * (1.0 / (2.0 * math.pi)) * moment)
        mc, ms = mc * scale, ms * scale

        def both(base, c, s):
            low_re, high_re = acc[base, 0, 0:8, lanes], acc[base, 0, 8:16, lanes]
            low_im, high_im = acc[base, 1, 0:8, lanes], acc[base, 1, 8:16, lanes]
            re = c * (low_re + high_re) + s * (low_im - high_im)
            im = c * (low_im + high_im) + s * (high_re - low_re)
            return re, im

        def late(re, im):
            a, b = mc * re + ms * im, mc * im - ms * re
            return a[0:4] + a[4:8], b[0:4] + b[4:8]

        zf = late(*both(0, tcf[0, Z_FACE : Z_FACE + 1, lanes], tcf[1, Z_FACE : Z_FACE + 1, lanes]))
        xf = late(*both(1, tb[0, CB : CB + 1, lanes], tb[1, CB : CB + 1, lanes]))
        c, s = tb[0, pl.ds(y_face, 1), lanes], tb[1, pl.ds(y_face, 1), lanes]
        re, im = acc[2, 0, 0:8, lanes], acc[2, 1, 0:8, lanes]
        yf = late(c * re - s * im, c * im + s * re)
        for k in range(2):
            z4, x4, y4 = zf[k], xf[k], yf[k]
            six = [
                z4[0:1] + y4[1:2], z4[1:2] + x4[0:1], x4[1:2] + y4[0:1],
                z4[2:3] + y4[3:4], z4[3:4] + x4[2:3], x4[3:4] + y4[2:3],
            ]
            for j, v in enumerate(six):
                rows48[12 * f + 6 * k + j : 12 * f + 6 * k + j + 1] = v
    rows48[48:128] = jnp.zeros((80, QN), F32)
    for t in range(0, QN, 128):
        send_buf[t : t + 128] = jnp.transpose(rows48[:, t : t + 128])

    second = []
    for d in range(1, GY):
        to = lax.rem(gy + d, GY)
        copy = pltpu.make_async_remote_copy(
            src_ref=send_buf.at[pl.ds(pl.multiple_of(to * OWN, OWN), OWN)],
            dst_ref=recv_buf.at[GY - d],
            send_sem=send2.at[d],
            recv_sem=recv2.at[GY - d],
            device_id=(gx, to),
            device_id_type=MESH,
        )
        copy.start()
        second.append(copy)
    total = send_buf[pl.ds(pl.multiple_of(gy * OWN, OWN), OWN)]
    for copy in second:
        copy.wait()
    for d in range(1, GY):
        total = total + recv_buf[d]
    far[...] = total[:, 0:48]


VMEM = pl.BlockSpec(memory_space=pltpu.VMEM)
SMEM = pl.BlockSpec(memory_space=pltpu.SMEM)
ANY = pl.BlockSpec(memory_space=pl.ANY)


def local(efield, hfield, e_coef, omega, patch_owner, patch_corner, surface_points, surface_faces, angle_index):
    field = jax.ShapeDtypeStruct((3, ROWS, CZ), F32)
    fields = [
        pltpu.VMEM((3, ROWS + CB, CZ), F32),
        pltpu.VMEM((3, ROWS + CB, CZ), F32),
        pltpu.VMEM((ROWS, CZ), F32),
        pltpu.VMEM((2, CB, CZ), F32),
        pltpu.VMEM((2, CB, CZ), F32),
    ]
    coef = e_coef.reshape(ROWS, CZ)
    efield, hfield, halo = pl.pallas_call(
        first_kernel,
        out_shape=(field, field, jax.ShapeDtypeStruct((9, CB, CZ), F32)),
        in_specs=[ANY, ANY, ANY],
        out_specs=(ANY, ANY, VMEM),
        scratch_shapes=fields
        + [
            pltpu.VMEM((2, 9, CB, CZ), F32),
            pltpu.VMEM((9, CB, CZ), F32),
            pltpu.SemaphoreType.DMA((3,)),
            pltpu.SemaphoreType.DMA((2, 6)),
            pltpu.SemaphoreType.DMA((2, 6)),
        ],
        compiler_params=pltpu.CompilerParams(collective_id=0, has_side_effects=True, vmem_limit_bytes=32 * 2**20),
        name="first_step",
    )(efield.reshape(3, ROWS, CZ), hfield.reshape(3, ROWS, CZ), coef)
    points = surface_points.reshape(SPB)
    faces = surface_faces.reshape(SPB)
    place = jnp.stack([points, faces])
    efield, hfield, sampled = pl.pallas_call(
        second_kernel,
        out_shape=(field, field, jax.ShapeDtypeStruct((16, SPB), F32)),
        in_specs=[SMEM, SMEM, SMEM, SMEM, VMEM, VMEM, ANY, ANY, ANY],
        out_specs=(ANY, ANY, VMEM),
        scratch_shapes=fields
        + [
            pltpu.VMEM((4 * SPB, CZ), F32),
            pltpu.SMEM((SLOTS + 1,), jnp.int32),
            pltpu.SMEM((SLOTS + 1,), jnp.int32),
            pltpu.SMEM((1,), jnp.int32),
            pltpu.SemaphoreType.DMA((3,)),
        ],
        compiler_params=pltpu.CompilerParams(vmem_limit_bytes=32 * 2**20),
        name="patches",
    )(patch_owner, patch_corner.reshape(-1), points, faces, place, halo, efield, hfield, coef)
    mine = lax.dynamic_slice(angle_index, (lax.axis_index("gx") * QN, 0), (QN, 2)).T
    far = pl.pallas_call(
        third_kernel,
        out_shape=jax.ShapeDtypeStruct((OWN, 48), F32),
        in_specs=[SMEM, VMEM, VMEM],
        out_specs=VMEM,
        scratch_shapes=[
            pltpu.VMEM((16, GX * SPB), F32),
            pltpu.VMEM((GX, 16, SPB), F32),
            pltpu.VMEM((8, QF), F32),
            pltpu.VMEM((2, 2 * XF, QF), BF16),
            pltpu.VMEM((2, 4 * ZF, QF), BF16),
            pltpu.VMEM((2, CB + 8, QF), F32),
            pltpu.VMEM((2, ZF, QF), F32),
            pltpu.VMEM((2 * XF, GX * SPB), BF16),
            pltpu.VMEM((YF_ROWS * 8, GX * SPB), BF16),
            pltpu.VMEM((YF_ROWS * 8, GX * SPB), BF16),
            pltpu.VMEM((2, YF_ROWS * 8, 2 * XF), BF16),
            pltpu.VMEM((2, YF_ROWS * 8, XF), BF16),
            pltpu.VMEM((2, CB * 16, 4 * ZF), BF16),
            pltpu.VMEM((2, YF_ROWS * 8, CHUNK), F32),
            pltpu.VMEM((3, 2, 16, QF), F32),
            pltpu.VMEM((128, QN), F32),
            pltpu.VMEM((QN, 128), F32),
            pltpu.VMEM((GY, OWN, 128), F32),
            pltpu.SemaphoreType.DMA((GX,)),
            pltpu.SemaphoreType.DMA((GX,)),
            pltpu.SemaphoreType.DMA((GY,)),
            pltpu.SemaphoreType.DMA((GY,)),
        ],
        compiler_params=pltpu.CompilerParams(collective_id=1, has_side_effects=True, vmem_limit_bytes=48 * 2**20),
        name="projection",
    )(omega, sampled, mine)
    shape = (3, CB, CB, CZ)
    return efield.reshape(shape), hfield.reshape(shape), far


def solution(mesh):
    placed = (
        P(None, "gx", "gy", None),
        P(None, "gx", "gy", None),
        P("gx", "gy", None),
        P(),
        P(),
        P(),
        P("gx", "gy", None),
        P("gx", "gy", None),
        P(),
    )
    return jax.shard_map(
        local,
        mesh=mesh,
        in_specs=placed,
        out_specs=(P(None, "gx", "gy", None), P(None, "gx", "gy", None), P(("gx", "gy"), None)),
        check_vma=False,
    )
```

time: 1590 us -> 84 us (0.05); the launches traced: 1570 us -> 83.7 us
  waiting for transfers between devices: 829 us -> 0 us
  matrix products: 401 us -> 0 us
  local copies, waits for them, and re-layouts: 215 us -> 7.29 us
  Pallas kernels: 0 us -> 75.6 us
  other arithmetic: 36 us -> 0.01 us
  loops' own time: 34.8 us -> 0 us
  starting transfers between devices: 34.4 us -> 0 us
  between operations: 22.9 us -> 0.77 us
    reduce_scatter x1 -> x0, waiting for transfers between devices: 730 us -> none  [local(): lax.psum_scatter(project_blocks(angle_index, omega, currents, positions,...]
    dot_general x146 -> x0, matrix products: 401 us -> none  [the longest x32 95.6 us: project(): jnp.dot(sine, imag_cur, precision=hp)]
    unnamed x81 -> x26, local copies, waits for them, and re-layouts: 108 us -> 7.15 us
    ppermute x8 -> x0, waiting for transfers between devices: 98.8 us -> none  [passed_along(): return lax.ppermute(block, axis, route)]
    pallas_call x0 -> x3, Pallas kernels: none -> 75.6 us  [the longest x1 36.4 us: local(): pl.pallas_call(third_kernel, out_shape=jax.ShapeDtypeStruct((OWN, 48), F3...]
    cond x46 -> x0, local copies, waits for them, and re-layouts: 41.7 us -> none  [the longest x2 32.8 us: local(): lax.cond(present, taken, lambda fields: fields, (efield, hfield))]
    another operation x9 -> x0, loops' own time: 34.8 us -> none  [the longest x8 34.3 us: local(): lax.cond(present, taken, lambda fields: fields, (efield, hfield))]
    ppermute x8 -> x0, starting transfers between devices: 34.3 us -> none  [passed_along(): return lax.ppermute(block, axis, route)]
  transfers between devices with their start and end apart: 9 -> 0, of which waited for: 4 -> 0; matrix products, arithmetic and copies ran while one was open for 6% -> 0% of each run, Pallas kernels for 0% -> 0%
where the time goes in v1:
time: 84 us; the launch traced here: 83.7 us
  Pallas kernels  75.6 us (90%)
  local copies, waits for them, and re-layouts  7.29 us (9%)
    pallas_call x1, Pallas kernels, local(): pl.pallas_call(third_kernel, out_shape=jax.ShapeDtypeStruct((OWN, 48), F3...  36.4 us
    pallas_call x1, Pallas kernels, local(): pl.pallas_call(first_kernel, out_shape=(field, field, jax.ShapeDtypeStruc...  25.3 us
    pallas_call x1, Pallas kernels, local(): pl.pallas_call(second_kernel, out_shape=(field, field, jax.ShapeDtypeStru...  13.9 us
    unnamed x26, local copies, waits for them, and re-layouts  7.15 us

profile of v1, /device:TPU:1, one launch (start us, length us, event | category | flops | bytes accessed | tf_op | source)
XLA Modules:
  0.0 83.7 jit_solution(15035300547929399783)
XLA Ops:
  0.6 0.0 copy-start
  0.6 0.0 copy-start.1
  0.7 1.0 %copy-done.1 = f32[32,32,128]{2,1,0:T(8,128)S(1)} copy-done((f32[32,32,128]{2,1,0:T(8,128)S(1)}, f32[32,32,128]{2,1,0:T(8,128)}, u32[]{:S(2)}) %copy-start.1) | copy-done | bytes 524312
  1.7 0.0 copy-start.3
  1.7 1.4 %copy-done.3 = f32[3,32,32,128]{3,2,1,0:T(8,128)S(1)} copy-done((f32[3,32,32,128]{3,2,1,0:T(8,128)S(1)}, f32[3,32,32,128]{3,2,1,0:T(8,128)}, u32[]{:S(2)}) %copy-start.3) | copy-done | bytes 1572888
  3.1 1.4 %copy-done.4 = f32[3,32,32,128]{3,2,1,0:T(8,128)S(1)} copy-done((f32[3,32,32,128]{3,2,1,0:T(8,128)S(1)}, f32[3,32,32,128]{3,2,1,0:T(8,128)}, u32[]{:S(2)}) %copy-start.4) | copy-done | bytes 1572888
  4.5 0.0 copy-start.10
  4.5 25.3 %first_step.1 = (f32[3,1024,128]{2,1,0:T(8,128)S(1)}, f32[3,1024,128]{2,1,0:T(8,128)S(1)}, f32[9,32,128]{2,1,0:T(8,128)S(1)}) custom-call(f32[3,1024,128]{2,1,0:T(8,128)S(1)} %bitcast.13, f32[3,1024,128]{2,1,0:T(8,128)S(1)} %bitcast.14, f32[1024,128]{1,0:T(8,128)S(1)} %bitcast.11), custom_call_target="tpu_custom_call" | custom-call | tf_op jit(solution)/shard_map/first_step/pallas_call | solution.py:729
  29.9 0.0 copy-start.5
  29.9 1.1 %copy-done.5 = f32[3,1024,128]{2,1,0:T(8,128)} copy-done((f32[3,1024,128]{2,1,0:T(8,128)}, f32[3,1024,128]{2,1,0:T(8,128)S(1)}, u32[]{:S(2)}) %copy-start.5) | copy-done | bytes 1572888
  31.0 0.0 copy-done.11
  31.0 0.1 copy.12
  31.1 0.1 reshape.30.corner
  31.3 0.0 copy-done.7
  31.3 0.0 copy-done.8
  31.3 0.0 copy-done.2
  31.3 0.0 copy-done.10
  31.3 0.0 copy-start.6
  31.3 1.4 %copy-done.6 = f32[3,1024,128]{2,1,0:T(8,128)S(1)} copy-done((f32[3,1024,128]{2,1,0:T(8,128)S(1)}, f32[3,1024,128]{2,1,0:T(8,128)}, u32[]{:S(2)}) %copy-start.6) | copy-done | bytes 1572888
  32.7 13.9 %patches.1 = (f32[3,1024,128]{2,1,0:T(8,128)}, f32[3,1024,128]{2,1,0:T(8,128)}, f32[16,256]{1,0:T(8,128)S(1)}) custom-call(s32[128]{0:T(128)S(1)} %copy-done.10, s32[256]{0:T(256)S(1)} %reshape.30.corner, s32[256]{0:T(256)S(1)} %bitcast.16, s32[256]{0:T(256)S(1)} %bitcast.18, s32[2,256]{1,0:T(2,128)S(1)} %pad_add_fusion.place, ...), custom_call_target="tpu_custom_call" | custom-call | tf_op jit(solution)/shard_map/patches/pallas_call | solution.py:748
  46.6 0.0 copy-done
  46.7 0.0 copy-done.9
  46.7 36.4 %projection.1 = f32[32,48]{1,0:T(8,128)S(1)} custom-call(f32[4]{0:T(128)S(1)} %copy-done.9, f32[16,256]{1,0:T(8,128)S(1)} %get-tuple-element.14.sampled, s32[2,512]{1,0:T(2,128)S(1)} %dynamic-slice_bitcast_fusion.angles), custom_call_target="tpu_custom_call" | custom-call | tf_op jit(solution)/shard_map/projection/pallas_call | solution.py:765
  83.1 0.6 copy.14
  (8 shorter events, 0.0 us)
Async XLA Ops:
  0.6 46.0 %copy-start = (s32[4096,2]{0,1:T(2,128)S(1)}, s32[4096,2]{0,1:T(2,128)}, u32[]{:S(2)}) copy-start(s32[4096,2]{0,1:T(2,128)} %param.17) | copy-start | bytes 98308
  0.6 1.0 %copy-start.1 = (f32[32,32,128]{2,1,0:T(8,128)S(1)}, f32[32,32,128]{2,1,0:T(8,128)}, u32[]{:S(2)}) copy-start(f32[32,32,128]{2,1,0:T(8,128)} %param.11) | copy-start | bytes 1572868
  1.7 1.4 %copy-start.3 = (f32[3,32,32,128]{3,2,1,0:T(8,128)S(1)}, f32[3,32,32,128]{3,2,1,0:T(8,128)}, u32[]{:S(2)}) copy-start(f32[3,32,32,128]{3,2,1,0:T(8,128)} %param.9) | copy-start | bytes 4718596
  3.1 1.4 %copy-start.4 = (f32[3,32,32,128]{3,2,1,0:T(8,128)S(1)}, f32[3,32,32,128]{3,2,1,0:T(8,128)}, u32[]{:S(2)}) copy-start(f32[3,32,32,128]{3,2,1,0:T(8,128)} %param.10) | copy-start | bytes 4718596
  4.5 26.5 %copy-start.11 = (s32[128,2]{0,1:T(2,128)S(1)}, s32[128,2]{0,1:T(2,128)}, u32[]{:S(2)}) copy-start(s32[128,2]{0,1:T(2,128)} %param.14) | copy-start | bytes 3076
  4.5 26.7 %copy-start.7 = (s32[1,1,256]{2,1,0:T(1,128)S(1)}, s32[1,1,256]{2,1,0:T(1,128)}, u32[]{:S(2)}) copy-start(s32[1,1,256]{2,1,0:T(1,128)} %param.15) | copy-start | bytes 3076
  4.5 26.8 %copy-start.8 = (s32[1,1,256]{2,1,0:T(1,128)S(1)}, s32[1,1,256]{2,1,0:T(1,128)}, u32[]{:S(2)}) copy-start(s32[1,1,256]{2,1,0:T(1,128)} %param.16) | copy-start | bytes 3076
  4.5 26.8 %copy-start.2 = (f32[32,32,128]{2,1,0:T(8,128)S(1)}, f32[32,32,128]{2,1,0:T(8,128)}, u32[]{:S(2)}) copy-start(f32[32,32,128]{2,1,0:T(8,128)} %param.11) | copy-start | bytes 1572868
  4.5 26.8 %copy-start.10 = (s32[128]{0:T(128)S(1)}, s32[128]{0:T(128)}, u32[]{:S(2)}) copy-start(s32[128]{0:T(128)} %owner.1) | copy-start | bytes 1540
  29.9 1.1 %copy-start.5 = (f32[3,1024,128]{2,1,0:T(8,128)}, f32[3,1024,128]{2,1,0:T(8,128)S(1)}, u32[]{:S(2)}) copy-start(f32[3,1024,128]{2,1,0:T(8,128)S(1)} %get-tuple-element.11.h_in) | copy-start | bytes 4718596
  31.3 1.4 %copy-start.6 = (f32[3,1024,128]{2,1,0:T(8,128)S(1)}, f32[3,1024,128]{2,1,0:T(8,128)}, u32[]{:S(2)}) copy-start(f32[3,1024,128]{2,1,0:T(8,128)} %copy-done.5) | copy-start | bytes 4718596
  32.7 13.9 %copy-start.9 = (f32[4]{0:T(128)S(1)}, f32[4]{0:T(128)}, u32[]{:S(2)}) copy-start(f32[4]{0:T(128)} %omega.1) | copy-start | bytes 52

commit v2 on v1

--- a/solution.py
+++ b/solution.py
@@ -93,29 +93,29 @@
 
 
 def advance(es, hs, cs, ye, yh):
-    def slab(x, carry):
-        r = pl.multiple_of(x * CB, CB)
-        here = pl.ds(r, CB)
-        after = pl.ds(pl.multiple_of(r + CB, CB), CB)
+    last = rows_of((CB, CZ)) == CB - 1
+    for x in range(CB):
+        r = x * CB
+        here, after = slice(r, r + CB), slice(r + CB, r + 2 * CB)
         ex, ey, ez = [es[k, here] for k in range(3)]
         ey1, ez1 = es[1, after], es[2, after]
         hx, hy, hz = [hs[k, after] for k in range(3)]
-        hy0, hz0 = hs[1, here], hs[2, here]
-        row = pl.ds(x, 1)
-        hx = hx - 0.5 * (y_next(ez, ye[1, row]) - ez - z_next(ey) + ey)
+        if x == 0:
+            hy0, hz0 = hs[1, here], hs[2, here]
+        exu = jnp.where(last, ye[0, x : x + 1], es[0, r + 1 : r + CB + 1])
+        ezu = jnp.where(last, ye[1, x : x + 1], es[2, r + 1 : r + CB + 1])
+        hx = hx - 0.5 * (ezu - ez - z_next(ey) + ey)
         hy = hy - 0.5 * (z_next(ex) - ex - ez1 + ez)
-        hz = hz - 0.5 * (ey1 - ey - y_next(ex, ye[0, row]) + ex)
-        c = cs[here]
-        ex = ex + c * (hz - y_prev(hz, yh[1, row]) - hy + z_prev(hy))
-        ey = ey + c * (hx - z_prev(hx) - hz + hz0)
-        ez = ez + c * (hy - hy0 - hx + y_prev(hx, yh[0, row]))
+        hz = hz - 0.5 * (ey1 - ey - exu + ex)
         for k, v in enumerate((hx, hy, hz)):
             hs[k, after] = v
+        c = cs[here]
+        ex = ex + c * (hz - y_prev(hz, yh[1, x : x + 1]) - hy + z_prev(hy))
+        ey = ey + c * (hx - z_prev(hx) - hz + hz0)
+        ez = ez + c * (hy - hy0 - hx + y_prev(hx, yh[0, x : x + 1]))
         for k, v in enumerate((ex, ey, ez)):
             es[k, here] = v
-        return carry
-
-    lax.fori_loop(0, CB, slab, 0)
+        hy0, hz0 = hy, hz
 
 
 def neighbours():
@@ -132,7 +132,85 @@
     return ref.at[8, pl.ds(8 * (n - 4), 8)]
 
 
-def first_kernel(e_in, h_in, c_in, e_out, h_out, halo2, es, hs, cs, ye, yh, sent, halo1, local_sem, send_sem, recv_sem):
+def fitted(function, degrees, points=4001):
+    r = np.cos(np.linspace(0.0, np.pi, points)) * 0.5
+    basis = np.stack([r**d for d in degrees], axis=1)
+    return [float(v) for v in np.linalg.lstsq(basis, function(np.pi * r) * math.sqrt(2.0), rcond=None)[0]]
+
+
+SIN = fitted(np.sin, (1, 3, 5, 7, 9))
+COS = fitted(np.cos, (0, 2, 4, 6, 8))
+
+
+def turn(t):
+    r = t - jnp.round(t)
+    r2 = r * r
+    s = r * (SIN[0] + r2 * (SIN[1] + r2 * (SIN[2] + r2 * (SIN[3] + r2 * SIN[4]))))
+    c = COS[0] + r2 * (COS[1] + r2 * (COS[2] + r2 * (COS[3] + r2 * COS[4])))
+    return 1.0 - s * s, s * c
+
+
+def split(v):
+    high = v.astype(BF16)
+    return high, (v - high.astype(F32)).astype(BF16)
+
+
+def dot(a, b):
+    return jnp.dot(a, b, preferred_element_type=F32)
+
+
+def dot_t(a, b):
+    return lax.dot_general(a, b, (((1,), (1,)), ((), ())), preferred_element_type=F32)
+
+
+CUT1 = 2
+CUT2 = 5
+XF = 128
+ZF = 64
+YF_ROWS = 96
+CHUNK = 256
+X_FACE = 111
+Z_FACE = 47
+
+
+def directions(omega, angles, kdir):
+    index = angles[...].astype(F32)
+    theta = math.pi * (index[0:1] + 0.5) / NTH
+    phi = 2.0 * math.pi * (index[1:2] + 0.5) / NPH
+    st, ct = jnp.sin(theta), jnp.cos(theta)
+    sp, cp = jnp.sin(phi), jnp.cos(phi)
+    for f in range(FREQ):
+        w = omega[f] * (1.0 / (2.0 * math.pi))
+        lanes = slice(f * QN, (f + 1) * QN)
+        kdir[0:1, lanes] = st * cp * w
+        kdir[1:2, lanes] = st * sp * w
+        kdir[2:3, lanes] = ct * w
+
+
+def tables(kdir, ta, tc, tb, tcf, n):
+    y_start = (lax.axis_index("gy") * CB).astype(F32) + (0.5 - CB * GY / 2.0)
+    lanes = pl.ds(pl.multiple_of(n * CHUNK, CHUNK), CHUNK)
+    kx, ky, kz = kdir[0:1, lanes], kdir[1:2, lanes], kdir[2:3, lanes]
+    count = rows_of((16, CHUNK)).astype(F32)
+    for j in range(0, XF, 16):
+        for k, v in enumerate(turn((count + (j + 0.5)) * kx)):
+            high, low = split(v)
+            ta[k, j : j + 16, lanes] = high
+            ta[k, XF + j : XF + j + 16, lanes] = low
+    for j in range(0, ZF, 16):
+        for k, v in enumerate(turn((count + (j + 0.5)) * kz)):
+            high, low = split(v)
+            tc[k, j : j + 16, lanes] = high
+            tc[k, ZF + j : ZF + j + 16, lanes] = low
+            tcf[k, j : j + 16, lanes] = v
+    for j in range(0, CB, 16):
+        for k, v in enumerate(turn((count + (y_start + j)) * ky)):
+            tb[k, j : j + 16, lanes] = v
+    for k, v in enumerate(turn(jnp.full((8, CHUNK), X_FACE + 0.5, F32) * kx)):
+        tb[k, CB : CB + 8, lanes] = v
+
+
+def first_kernel(omega, angles, e_in, h_in, c_in, e_out, h_out, halo2, ta_out, tc_out, tb_out, tcf_out, kdir, ta, tc, tb, tcf, es, hs, cs, ye, yh, sent, halo1, local_sem, send_sem, recv_sem):
     loads = [
         pltpu.make_async_copy(e_in, es.at[:, pl.ds(0, ROWS)], local_sem.at[0]),
         pltpu.make_async_copy(h_in, hs.at[:, pl.ds(CB, ROWS)], local_sem.at[1]),
@@ -143,6 +221,16 @@
     barrier = pltpu.get_barrier_semaphore()
     for device in neighbours():
         pl.semaphore_signal(barrier, inc=1, device_id=device, device_id_type=MESH)
+    directions(omega, angles, kdir)
+
+    def some_tables(low, high):
+        def one(n, carry):
+            tables(kdir, ta, tc, tb, tcf, n)
+            return carry
+
+        lax.fori_loop(low, high, one, 0)
+
+    some_tables(0, CUT1)
     loads[0].wait()
     loads[1].wait()
 
@@ -164,6 +252,7 @@
     prepare(es, hs, sent.at[0])
     pl.semaphore_wait(barrier, 6)
     copies = exchange(0, halo1)
+    some_tables(CUT1, CUT2)
     loads[2].wait()
     for copy in copies:
         copy.wait()
@@ -177,6 +266,11 @@
     ]
     for copy in stores:
         copy.start()
+    some_tables(CUT2, QF // CHUNK)
+    for n, (table, out) in enumerate(((ta, ta_out), (tc, tc_out), (tb, tb_out), (tcf, tcf_out))):
+        copy = pltpu.make_async_copy(table, out, local_sem.at[2 + n])
+        copy.start()
+        stores.append(copy)
     for copy in copies + stores:
         copy.wait()
 
@@ -318,7 +412,7 @@
         hs[k, pl.ds((x0 + i + 1) * CB + y0, PB)] = h_new[k]
 
 
-def second_kernel(owner, corner, points, faces, place, halo, e_in, h_in, c_in, e_out, h_out, sampled, es, hs, cs, ye, yh, taken, slot_x, slot_y, count, sem):
+def second_kernel(owner, corner, spots, place, halo, e_in, h_in, c_in, e_out, h_out, sampled, es, hs, cs, ye, yh, taken, slot_x, slot_y, count, sem):
     loads = [
         pltpu.make_async_copy(e_in, es.at[:, pl.ds(0, ROWS)], sem.at[0]),
         pltpu.make_async_copy(h_in, hs.at[:, pl.ds(CB, ROWS)], sem.at[1]),
@@ -346,24 +440,22 @@
         lax.fori_loop(0, count[0], one, 0)
 
     def sample():
+        e_rows = es.reshape(3 * (ROWS + CB), CZ)
+        h_rows = hs.reshape(3 * (ROWS + CB), CZ)
+
         def one(n, carry):
-            cell = jnp.maximum(points[n], 0)
-            row = cell // CZ
-            mask = lane == cell % CZ
-            k = faces[n] // 2
-            k1 = jnp.where(k == 2, 0, k + 1)
-            k2 = jnp.where(k == 0, 2, k - 1)
-            taken[pl.ds(n + 0 * SPB, 1)] = jnp.where(mask, hs[k1, pl.ds(row + CB, 1)], 0.0)
-            taken[pl.ds(n + 1 * SPB, 1)] = jnp.where(mask, hs[k2, pl.ds(row + CB, 1)], 0.0)
-            taken[pl.ds(n + 2 * SPB, 1)] = jnp.where(mask, es[k1, pl.ds(row, 1)], 0.0)
-            taken[pl.ds(n + 3 * SPB, 1)] = jnp.where(mask, es[k2, pl.ds(row, 1)], 0.0)
+            mask = lane == spots[n]
+            k1, k2 = spots[SPB + n], spots[2 * SPB + n]
+            taken[pl.ds(n, 1)] = jnp.where(mask, h_rows[pl.ds(k1 + CB, 1)], 0.0)
+            taken[pl.ds(n + SPB, 1)] = jnp.where(mask, h_rows[pl.ds(k2 + CB, 1)], 0.0)
+            taken[pl.ds(n + 2 * SPB, 1)] = jnp.where(mask, e_rows[pl.ds(k1, 1)], 0.0)
+            taken[pl.ds(n + 3 * SPB, 1)] = jnp.where(mask, e_rows[pl.ds(k2, 1)], 0.0)
             return carry
 
-        lax.fori_loop(0, SPB, one, 0, unroll=8)
-        return lax.dot_general(
-            jnp.ones((8, CZ), F32), taken[...], (((1,), (1,)), ((), ())),
-            precision=lax.Precision.HIGHEST, preferred_element_type=F32,
-        )
+        lax.fori_loop(0, SPB, one, 0, unroll=16)
+        high, low = split(taken[...])
+        ones = jnp.ones((16, CZ), BF16)
+        return dot_t(ones, high) + dot_t(ones, low)
 
     slots = place[0:1]
     face = place[1:2]
@@ -396,53 +488,24 @@
         copy.wait()
 
 
-def fitted(function, degrees, points=4001):
-    r = np.cos(np.linspace(0.0, np.pi, points)) * 0.5
-    basis = np.stack([r**d for d in degrees], axis=1)
-    return [float(v) for v in np.linalg.lstsq(basis, function(np.pi * r) * math.sqrt(2.0), rcond=None)[0]]
-
-
-SIN = fitted(np.sin, (1, 3, 5, 7, 9))
-COS = fitted(np.cos, (0, 2, 4, 6, 8))
-
-
-def turn(t):
-    r = t - jnp.round(t)
-    r2 = r * r
-    s = r * (SIN[0] + r2 * (SIN[1] + r2 * (SIN[2] + r2 * (SIN[3] + r2 * SIN[4]))))
-    c = COS[0] + r2 * (COS[1] + r2 * (COS[2] + r2 * (COS[3] + r2 * COS[4])))
-    return 1.0 - s * s, s * c
-
-
-def split(v):
-    high = v.astype(BF16)
-    return high, (v - high.astype(F32)).astype(BF16)
-
-
-def dot(a, b):
-    return jnp.dot(a, b, preferred_element_type=F32)
-
-
-def dot_t(a, b):
-    return lax.dot_general(a, b, (((1,), (1,)), ((), ())), preferred_element_type=F32)
-
-
-XF = 128
-ZF = 64
-YF_ROWS = 96
-CHUNK = 256
-X_FACE = 111
-Z_FACE = 47
-
-
-def third_kernel(omega, sampled, angles, far, got, gathered, kdir, ta, tc, tb, tcf, hot, spread_hi, spread_lo, lhs1, lhs2, lhsz, big, acc, rows48, send_buf, recv_buf, send1, recv1, send2, recv2):
+def third_kernel(omega, sampled, ta_in, tc_in, tb_in, tcf_in, far, got, gathered, ta, tc, tb, tcf, hot, hotz, spread_hi, spread_lo, lhs1, lhs2, lhsz, acc, rows48, send_buf, recv_buf, load_sem, send1, recv1, send2, recv2):
     gx = lax.axis_index("gx")
     gy = lax.axis_index("gy")
+    loads = [
+        pltpu.make_async_copy(ta_in, ta, load_sem.at[0]),
+        pltpu.make_async_copy(tc_in, tc.at[:, pl.ds(0, 2 * ZF)], load_sem.at[1]),
+        pltpu.make_async_copy(tc_in.at[:, pl.ds(0, ZF)], tc.at[:, pl.ds(2 * ZF, ZF)], load_sem.at[2]),
+        pltpu.make_async_copy(tb_in, tb, load_sem.at[3]),
+        pltpu.make_async_copy(tcf_in, tcf, load_sem.at[4]),
+    ]
+    for copy in loads:
+        copy.start()
     barrier = pltpu.get_barrier_semaphore()
     for d in range(1, GX):
         pl.semaphore_signal(barrier, inc=1, device_id=(lax.rem(gx + d, GX), gy), device_id_type=MESH)
     for d in range(1, GY):
         pl.semaphore_signal(barrier, inc=1, device_id=(gx, lax.rem(gy + d, GY)), device_id_type=MESH)
+    tc[:, 3 * ZF : 4 * ZF] = jnp.zeros((2, ZF, QF), BF16)
     pl.semaphore_wait(barrier, GX + GY - 2)
     first = []
     for d in range(1, GX):
@@ -456,48 +519,6 @@
         )
         copy.start()
         first.append(copy)
-
-    index = angles[...].astype(F32)
-    theta = math.pi * (index[0:1] + 0.5) / NTH
-    phi = 2.0 * math.pi * (index[1:2] + 0.5) / NPH
-    st, ct = jnp.sin(theta), jnp.cos(theta)
-    sp, cp = jnp.sin(phi), jnp.cos(phi)
-    for f in range(FREQ):
-        w = omega[f] * (1.0 / (2.0 * math.pi))
-        kdir[0:1, f * QN : (f + 1) * QN] = st * cp * w
-        kdir[1:2, f * QN : (f + 1) * QN] = st * sp * w
-        kdir[2:3, f * QN : (f + 1) * QN] = ct * w
-
-    y_start = (gy * CB).astype(F32) + (0.5 - CB * GY / 2.0)
-
-    def tables(n, carry):
-        lanes = pl.ds(pl.multiple_of(n * CHUNK, CHUNK), CHUNK)
-        kx, ky, kz = kdir[0:1, lanes], kdir[1:2, lanes], kdir[2:3, lanes]
-        for j in range(0, XF, 16):
-            at = rows_of((16, CHUNK)).astype(F32) + (j + 0.5)
-            for k, v in enumerate(turn(at * kx)):
-                high, low = split(v)
-                ta[k, j : j + 16, lanes] = high
-                ta[k, XF + j : XF + j + 16, lanes] = low
-        for j in range(0, ZF, 16):
-            at = rows_of((16, CHUNK)).astype(F32) + (j + 0.5)
-            for k, v in enumerate(turn(at * kz)):
-                high, low = split(v)
-                tc[k, j : j + 16, lanes] = high
-                tc[k, ZF + j : ZF + j + 16, lanes] = low
-                tc[k, 2 * ZF + j : 2 * ZF + j + 16, lanes] = high
-                tc[k, 3 * ZF + j : 3 * ZF + j + 16, lanes] = jnp.zeros((16, CHUNK), BF16)
-                tcf[k, j : j + 16, lanes] = v
-        for j in range(0, CB, 16):
-            at = rows_of((16, CHUNK)).astype(F32) + (y_start + j)
-            for k, v in enumerate(turn(at * ky)):
-                tb[k, j : j + 16, lanes] = v
-        at = jnp.full((8, CHUNK), X_FACE + 0.5, F32)
-        for k, v in enumerate(turn(at * kx)):
-            tb[k, CB : CB + 8, lanes] = v
-        return carry
-
-    lax.fori_loop(0, QF // CHUNK, tables, 0)
     gathered[0] = sampled[...]
     for copy in first:
         copy.wait()
@@ -513,146 +534,169 @@
         got[14:15, lanes] = jnp.where(z < 64.0, 63.0 - z, z - 64.0)
         got[15:16, lanes] = jnp.where(z < 64.0, -1.0, 1.0)
 
-    slots = GX * SPB
-
-    def one_hot(place_row, sign_row, count):
+    def one_hot(to, place_row, sign_row, count, blocks):
+        for b, start in enumerate(blocks):
+            lanes = pl.ds(start, SPB)
+            there = slice(b * SPB, (b + 1) * SPB)
+            where_at = jnp.broadcast_to(got[place_row : place_row + 1, lanes], (16, SPB))
+            sign = jnp.broadcast_to(got[sign_row : sign_row + 1, lanes], (16, SPB))
+            at = rows_of((16, SPB)).astype(F32)
+            for j in range(0, count, 16):
+                same = at + float(j) == where_at
+                to[j : j + 16, there] = jnp.where(same, 1.0, 0.0).astype(BF16)
+                to[count + j : count + j + 16, there] = jnp.where(same, sign, 0.0).astype(BF16)
+
+    def halves(v):
+        high = v.astype(BF16).astype(F32)
+        return high, v - high
+
+    def spread(v, key, start, step, first_row, there, count):
+        high, low = halves(v)
+
+        def one(n, carry):
+            same = key == (start + step * n).astype(F32)
+            at = pl.ds(pl.multiple_of(first_row + n * 16, 16), 16)
+            spread_hi[at, there] = jnp.where(same, high, 0.0).astype(BF16)
+            spread_lo[at, there] = jnp.where(same, low, 0.0).astype(BF16)
+            return carry
+
+        lax.fori_loop(0, count, one, 0, unroll=8)
+
+    def row16(row, lanes):
+        return jnp.broadcast_to(got[row : row + 1, lanes], (16, SPB))
+
+    upper = rows_of((16, SPB)) // 8
+    every = [b * SPB for b in range(GX)]
+    ends = [pl.multiple_of(lax.rem(GX - gx, GX) * SPB, SPB), pl.multiple_of((GX - 1 - gx) * SPB, SPB)]
+
+    def twice(lanes):
+        v = got[0:8, lanes]
+        return jnp.concatenate([v, v], axis=0)
+
+    def spread_z(y_low, count):
+        wanted = (4 + upper).astype(F32)
         for b in range(GX):
             lanes = slice(b * SPB, (b + 1) * SPB)
-            where_at = got[place_row : place_row + 1, lanes]
-            sign = got[sign_row : sign_row + 1, lanes]
-            for j in range(0, count, 16):
-                at = rows_of((16, SPB)).astype(F32) + float(j)
-                same = at == where_at
-                hot[j : j + 16, lanes] = jnp.where(same, 1.0, 0.0).astype(BF16)
-                hot[count + j : count + j + 16, lanes] = jnp.where(same, sign, 0.0).astype(BF16)
-
-    def spread(low_face, high_face):
-        for b in range(GX):
-            lanes = slice(b * SPB, (b + 1) * SPB)
-            cols = got[0:8, lanes]
-            face = got[11:12, lanes]
-            v = jnp.concatenate([jnp.where(face == low_face, cols, 0.0), jnp.where(face == high_face, cols, 0.0)], axis=0)
-            high = v.astype(BF16).astype(F32)
-            low = v - high
-            ys = got[9:10, lanes]
-
-            def one(y, carry):
-                same = ys == y.astype(F32)
-                at = pl.ds(pl.multiple_of(y * 16, 16), 16)
-                spread_hi[at, lanes] = jnp.where(same, high, 0.0).astype(BF16)
-                spread_lo[at, lanes] = jnp.where(same, low, 0.0).astype(BF16)
-                return carry
-
-            lax.fori_loop(0, CB, one, 0, unroll=4)
+            v = jnp.where(row16(11, lanes) == wanted, twice(lanes), 0.0)
+            spread(v, row16(9, lanes), y_low, 1, 0, lanes, count)
+
+    def spread_x(y_low, count):
+        for e, start in enumerate(ends):
+            lanes = pl.ds(start, SPB)
+            wanted = jnp.where(upper == e, float(e), -1.0)
+            v = jnp.where(row16(11, lanes) == wanted, twice(lanes), 0.0)
+            spread(v, row16(9, lanes), y_low, 1, 0, slice(e * SPB, (e + 1) * SPB), count)
 
     def spread_y():
         for b in range(GX):
             lanes = slice(b * SPB, (b + 1) * SPB)
-            face = got[11:12, lanes]
-            v = jnp.where((face == 2.0) | (face == 3.0), got[0:8, lanes], 0.0)
-            v = jnp.concatenate([v, v], axis=0)
-            high = v.astype(BF16).astype(F32)
-            low = v - high
-            zs = got[10:11, lanes]
-            second = (rows_of((16, SPB)) // 8).astype(F32)
-
-            def one(o, carry):
-                same = zs == second + (2 * o + 16).astype(F32)
-                at = pl.ds(pl.multiple_of(o * 16, 16), 16)
-                spread_hi[at, lanes] = jnp.where(same, high, 0.0).astype(BF16)
-                spread_lo[at, lanes] = jnp.where(same, low, 0.0).astype(BF16)
-                return carry
-
-            lax.fori_loop(0, YF_ROWS // 2, one, 0, unroll=4)
-
-    def dense(count):
-        for m in range(0, count, CHUNK):
+            face = row16(11, lanes)
+            v = jnp.where((face == 2.0) | (face == 3.0), twice(lanes), 0.0)
+            spread(v, row16(10, lanes) - upper.astype(F32), 16, 2, 0, lanes, YF_ROWS // 2)
+
+    def dense(to, rows):
+        for m in range(0, rows, CHUNK):
             d = dot_t(spread_hi[m : m + CHUNK], hot[...]) + dot_t(spread_lo[m : m + CHUNK], hot[...])
             for k in range(2):
                 high, low = split(d[:, k * XF : (k + 1) * XF])
-                lhs1[k, m : m + CHUNK, 0:XF] = high
-                lhs1[k, m : m + CHUNK, XF : 2 * XF] = high
-                lhs2[k, m : m + CHUNK] = low
-
-    one_hot(12, 13, XF)
-    spread(4.0, 5.0)
-    dense(CB * 16)
-
-    def outer_y(n, base):
-        lanes = pl.ds(pl.multiple_of(n * CHUNK, CHUNK), CHUNK)
-
-        def one(y, total):
-            re, im = total
-            at = pl.ds(pl.multiple_of(y * 16, 16), 16)
-            g_re, g_im = big[0, at], big[1, at]
-            bc, bs = tb[0, pl.ds(y, 1), lanes], tb[1, pl.ds(y, 1), lanes]
-            return re + (bc * g_re - bs * g_im), im + (bc * g_im + bs * g_re)
-
-        zero = jnp.zeros((16, CHUNK), F32)
-        re, im = lax.fori_loop(0, CB, one, (zero, zero), unroll=4)
-        acc[base, 0, :, lanes] = re
-        acc[base, 1, :, lanes] = im
-
-    def across_z(n, carry):
-        lanes = pl.ds(pl.multiple_of(n * CHUNK, CHUNK), CHUNK)
+                lhs1[k, to + m : to + m + CHUNK, 0:XF] = high
+                lhs1[k, to + m : to + m + CHUNK, XF : 2 * XF] = high
+                lhs2[k, to + m : to + m + CHUNK] = low
+
+    def dense_x(rows):
+        for m in range(0, rows, CHUNK):
+            at = slice(m, m + CHUNK)
+            d = dot_t(spread_hi[at, 0 : 2 * SPB], hotz[...]) + dot_t(spread_lo[at, 0 : 2 * SPB], hotz[...])
+            for k in range(2):
+                high, low = split(d[:, k * ZF : (k + 1) * ZF])
+                lhsz[k, at] = jnp.concatenate([high, high, low, jnp.zeros_like(low)], axis=1)
+
+    def times_x(to, lanes):
+        out = []
         for k in range(2):
             table = ta[k, :, lanes]
-            big[k, 0 : CB * 16] = dot(lhs1[k, 0 : CB * 16], table) + dot(lhs2[k, 0 : CB * 16], table[0:XF])
-        outer_y(n, 0)
-        return carry
-
-    lax.fori_loop(0, QF // CHUNK, across_z, 0)
+            out.append(dot(lhs1[k, to : to + CHUNK], table) + dot(lhs2[k, to : to + CHUNK], table[0:XF]))
+        return out
+
+    def times_z(to, lanes):
+        return [dot(lhsz[k, to : to + CHUNK], tc[k, :, lanes]) for k in range(2)]
+
+    def outer_y(g, total, y_low, lanes):
+        re, im = total
+        for y in range(16):
+            at = slice(y * 16, (y + 1) * 16)
+            bc, bs = tb[0, pl.ds(y_low + y, 1), lanes], tb[1, pl.ds(y_low + y, 1), lanes]
+            re = re + (bc * g[0][at] - bs * g[1][at])
+            im = im + (bc * g[1][at] + bs * g[0][at])
+        return re, im
+
+    def outer_z(g, total, z_low, lanes):
+        re, im = total
+        for o in range(CHUNK // 8):
+            z = z_low + o
+            j, sign = (z - 64, 1.0) if z >= 64 else (63 - z, -1.0)
+            at = slice(o * 8, (o + 1) * 8)
+            cc, cs = tcf[0, j : j + 1, lanes], sign * tcf[1, j : j + 1, lanes]
+            re = re + (cc * g[0][at] - cs * g[1][at])
+            im = im + (cc * g[1][at] + cs * g[0][at])
+        return re, im
+
+    def keep(base, total, lanes):
+        n = total[0].shape[0]
+        acc[base, 0, 0:n, lanes] = total[0]
+        acc[base, 1, 0:n, lanes] = total[1]
+
     edge = (gy == 0) | (gy == GY - 1)
+    zero16 = jnp.zeros((16, CHUNK), F32)
+    zero8 = jnp.zeros((8, CHUNK), F32)
+    one_hot(hot, 12, 13, XF, every)
+    one_hot(hotz, 14, 15, ZF, ends)
+    for copy in loads:
+        copy.wait()
 
     @pl.when(jnp.logical_not(edge))
     def _():
+        spread_z(0, CB)
+        dense(0, CB * 16)
+        spread_x(0, CB)
+        dense_x(CB * 16)
         acc[2] = jnp.zeros((2, 16, QF), F32)
+
+        def chunk(n, carry):
+            lanes = pl.ds(pl.multiple_of(n * CHUNK, CHUNK), CHUNK)
+            total = (zero16, zero16)
+            for y in range(2):
+                total = outer_y(times_x(y * CHUNK, lanes), total, y * 16, lanes)
+            keep(0, total, lanes)
+            total = (zero16, zero16)
+            for y in range(2):
+                total = outer_y(times_z(y * CHUNK, lanes), total, y * 16, lanes)
+            keep(1, total, lanes)
+            return carry
+
+        lax.fori_loop(0, QF // CHUNK, chunk, 0)
 
     @pl.when(edge)
     def _():
+        y_low = jnp.where(gy == 0, 16, 0)
+        spread_z(y_low, 16)
+        dense(0, CHUNK)
+        spread_x(y_low, 16)
+        dense_x(CHUNK)
         spread_y()
-        dense(YF_ROWS * 8)
-
-        def across_y(n, carry):
+        dense(CHUNK, YF_ROWS * 8)
+
+        def chunk(n, carry):
             lanes = pl.ds(pl.multiple_of(n * CHUNK, CHUNK), CHUNK)
-            for k in range(2):
-                table = ta[k, :, lanes]
-                big[k] = dot(lhs1[k], table) + dot(lhs2[k], table[0:XF])
-
-            def one(o, total):
-                re, im = total
-                below = pl.ds(pl.multiple_of((Z_FACE - o) * 8, 8), 8)
-                above = pl.ds(pl.multiple_of((Z_FACE + 1 + o) * 8, 8), 8)
-                cc, cs = tcf[0, pl.ds(o, 1), lanes], tcf[1, pl.ds(o, 1), lanes]
-                a_re, a_im, b_re, b_im = big[0, above], big[1, above], big[0, below], big[1, below]
-                re = re + (cc * (a_re + b_re) - cs * (a_im - b_im))
-                im = im + (cc * (a_im + b_im) + cs * (a_re - b_re))
-                return re, im
-
-            zero = jnp.zeros((8, CHUNK), F32)
-            re, im = lax.fori_loop(0, YF_ROWS // 2, one, (zero, zero), unroll=4)
-            acc[2, 0, 0:8, lanes] = re
-            acc[2, 1, 0:8, lanes] = im
+            keep(0, outer_y(times_x(0, lanes), (zero16, zero16), y_low, lanes), lanes)
+            keep(1, outer_y(times_z(0, lanes), (zero16, zero16), y_low, lanes), lanes)
+            total = (zero8, zero8)
+            for z in range(0, YF_ROWS, CHUNK // 8):
+                total = outer_z(times_x(CHUNK + z * 8, lanes), total, z + 16, lanes)
+            keep(2, total, lanes)
             return carry
 
-        lax.fori_loop(0, QF // CHUNK, across_y, 0)
-
-    one_hot(14, 15, ZF)
-    spread(0.0, 1.0)
-    for m in range(0, CB * 16, CHUNK):
-        d = dot_t(spread_hi[m : m + CHUNK], hot[0 : 2 * ZF]) + dot_t(spread_lo[m : m + CHUNK], hot[0 : 2 * ZF])
-        for k in range(2):
-            high, low = split(d[:, k * ZF : (k + 1) * ZF])
-            lhsz[k, m : m + CHUNK] = jnp.concatenate([high, high, low, jnp.zeros_like(low)], axis=1)
-
-    def across_x(n, carry):
-        lanes = pl.ds(pl.multiple_of(n * CHUNK, CHUNK), CHUNK)
-        for k in range(2):
-            big[k, 0 : CB * 16] = dot(lhsz[k], tc[k, :, lanes])
-        outer_y(n, 1)
-        return carry
-
-    lax.fori_loop(0, QF // CHUNK, across_x, 0)
+        lax.fori_loop(0, QF // CHUNK, chunk, 0)
 
     scale = 1.0 / math.sqrt(GX * GY * SPB)
     y_face = jnp.where(gy == 0, 16, 15)
@@ -726,29 +770,51 @@
         pltpu.VMEM((2, CB, CZ), F32),
     ]
     coef = e_coef.reshape(ROWS, CZ)
-    efield, hfield, halo = pl.pallas_call(
+    mine = lax.dynamic_slice(angle_index, (lax.axis_index("gx") * QN, 0), (QN, 2)).T
+    efield, hfield, halo, *tabled = pl.pallas_call(
         first_kernel,
-        out_shape=(field, field, jax.ShapeDtypeStruct((9, CB, CZ), F32)),
-        in_specs=[ANY, ANY, ANY],
-        out_specs=(ANY, ANY, VMEM),
-        scratch_shapes=fields
+        out_shape=(
+            field,
+            field,
+            jax.ShapeDtypeStruct((9, CB, CZ), F32),
+            jax.ShapeDtypeStruct((2, 2 * XF, QF), BF16),
+            jax.ShapeDtypeStruct((2, 2 * ZF, QF), BF16),
+            jax.ShapeDtypeStruct((2, CB + 8, QF), F32),
+            jax.ShapeDtypeStruct((2, ZF, QF), F32),
+        ),
+        in_specs=[SMEM, VMEM, ANY, ANY, ANY],
+        out_specs=(ANY, ANY, VMEM, ANY, ANY, ANY, ANY),
+        scratch_shapes=[
+            pltpu.VMEM((8, QF), F32),
+            pltpu.VMEM((2, 2 * XF, QF), BF16),
+            pltpu.VMEM((2, 2 * ZF, QF), BF16),
+            pltpu.VMEM((2, CB + 8, QF), F32),
+            pltpu.VMEM((2, ZF, QF), F32),
+        ]
+        + fields
         + [
             pltpu.VMEM((2, 9, CB, CZ), F32),
             pltpu.VMEM((9, CB, CZ), F32),
-            pltpu.SemaphoreType.DMA((3,)),
+            pltpu.SemaphoreType.DMA((6,)),
             pltpu.SemaphoreType.DMA((2, 6)),
             pltpu.SemaphoreType.DMA((2, 6)),
         ],
-        compiler_params=pltpu.CompilerParams(collective_id=0, has_side_effects=True, vmem_limit_bytes=32 * 2**20),
+        compiler_params=pltpu.CompilerParams(collective_id=0, has_side_effects=True, vmem_limit_bytes=56 * 2**20),
         name="first_step",
-    )(efield.reshape(3, ROWS, CZ), hfield.reshape(3, ROWS, CZ), coef)
+    )(omega, mine, efield.reshape(3, ROWS, CZ), hfield.reshape(3, ROWS, CZ), coef)
     points = surface_points.reshape(SPB)
     faces = surface_faces.reshape(SPB)
     place = jnp.stack([points, faces])
+    cell = jnp.maximum(points, 0)
+    normal = faces // 2
+    span = ROWS + CB
+    first_row = jnp.where(normal == 2, 0, normal + 1) * span + cell // CZ
+    second_row = jnp.where(normal == 0, 2, normal - 1) * span + cell // CZ
+    spots = jnp.concatenate([cell % CZ, first_row, second_row])
     efield, hfield, sampled = pl.pallas_call(
         second_kernel,
         out_shape=(field, field, jax.ShapeDtypeStruct((16, SPB), F32)),
-        in_specs=[SMEM, SMEM, SMEM, SMEM, VMEM, VMEM, ANY, ANY, ANY],
+        in_specs=[SMEM, SMEM, SMEM, VMEM, VMEM, ANY, ANY, ANY],
         out_specs=(ANY, ANY, VMEM),
         scratch_shapes=fields
         + [
@@ -758,42 +824,41 @@
             pltpu.SMEM((1,), jnp.int32),
             pltpu.SemaphoreType.DMA((3,)),
         ],
-        compiler_params=pltpu.CompilerParams(vmem_limit_bytes=32 * 2**20),
+        compiler_params=pltpu.CompilerParams(vmem_limit_bytes=56 * 2**20),
         name="patches",
-    )(patch_owner, patch_corner.reshape(-1), points, faces, place, halo, efield, hfield, coef)
-    mine = lax.dynamic_slice(angle_index, (lax.axis_index("gx") * QN, 0), (QN, 2)).T
+    )(patch_owner, patch_corner.reshape(-1), spots, place, halo, efield, hfield, coef)
     far = pl.pallas_call(
         third_kernel,
         out_shape=jax.ShapeDtypeStruct((OWN, 48), F32),
-        in_specs=[SMEM, VMEM, VMEM],
+        in_specs=[SMEM, VMEM, ANY, ANY, ANY, ANY],
         out_specs=VMEM,
         scratch_shapes=[
             pltpu.VMEM((16, GX * SPB), F32),
             pltpu.VMEM((GX, 16, SPB), F32),
-            pltpu.VMEM((8, QF), F32),
             pltpu.VMEM((2, 2 * XF, QF), BF16),
             pltpu.VMEM((2, 4 * ZF, QF), BF16),
             pltpu.VMEM((2, CB + 8, QF), F32),
             pltpu.VMEM((2, ZF, QF), F32),
             pltpu.VMEM((2 * XF, GX * SPB), BF16),
+            pltpu.VMEM((2 * ZF, 2 * SPB), BF16),
             pltpu.VMEM((YF_ROWS * 8, GX * SPB), BF16),
             pltpu.VMEM((YF_ROWS * 8, GX * SPB), BF16),
-            pltpu.VMEM((2, YF_ROWS * 8, 2 * XF), BF16),
-            pltpu.VMEM((2, YF_ROWS * 8, XF), BF16),
+            pltpu.VMEM((2, YF_ROWS * 8 + CHUNK, 2 * XF), BF16),
+            pltpu.VMEM((2, YF_ROWS * 8 + CHUNK, XF), BF16),
             pltpu.VMEM((2, CB * 16, 4 * ZF), BF16),
-            pltpu.VMEM((2, YF_ROWS * 8, CHUNK), F32),
             pltpu.VMEM((3, 2, 16, QF), F32),
             pltpu.VMEM((128, QN), F32),
             pltpu.VMEM((QN, 128), F32),
             pltpu.VMEM((GY, OWN, 128), F32),
+            pltpu.SemaphoreType.DMA((5,)),
             pltpu.SemaphoreType.DMA((GX,)),
             pltpu.SemaphoreType.DMA((GX,)),
             pltpu.SemaphoreType.DMA((GY,)),
             pltpu.SemaphoreType.DMA((GY,)),
         ],
-        compiler_params=pltpu.CompilerParams(collective_id=1, has_side_effects=True, vmem_limit_bytes=48 * 2**20),
+        compiler_params=pltpu.CompilerParams(collective_id=1, has_side_effects=True, vmem_limit_bytes=56 * 2**20),
         name="projection",
-    )(omega, sampled, mine)
+    )(omega, sampled, *tabled)
     shape = (3, CB, CB, CZ)
     return efield.reshape(shape), hfield.reshape(shape), far
 

time: 84 us -> 67.1 us (0.80)
  the two profiles are of different devices: /device:TPU:1 before, /device:TPU:27 now
where the time goes in v2:
time: 67.1 us; the launch traced here: 66.7 us
  Pallas kernels  58.7 us (87%)
  other arithmetic  3.97 us (6%)
  local copies, waits for them, and re-layouts  3.37 us (5%)
  between operations  0.68 us (1%)
    pallas_call x1, Pallas kernels, local(): pl.pallas_call(third_kernel, out_shape=jax.ShapeDtypeStruct((OWN, 48), F3...  30.9 us
    pallas_call x1, Pallas kernels, local(): pl.pallas_call(first_kernel, out_shape=(field, field, jax.ShapeDtypeStruc...  18.6 us
    pallas_call x1, Pallas kernels, local(): pl.pallas_call(second_kernel, out_shape=(field, field, jax.ShapeDtypeStru...  9.22 us
    unnamed x4, local copies, waits for them, and re-layouts  2.12 us

profile of v2, /device:TPU:27, one launch (start us, length us, event | category | flops | bytes accessed | tf_op | source)
XLA Modules:
  0.0 66.7 jit_solution(14994367013644704064)
XLA Ops:
  0.6 0.0 copy-start
  0.7 0.7 %compare_reduce_fusion = pred[256]{0:T(512)(128)(4,1)S(1)} fusion(s32[1,1,256]{2,1,0:T(1,128)} %param.15), kind=kLoop, calls=%fused_computation.2 | loop fusion | flops 768 | bytes 1280 | tf_op jit(solution)/shard_map/jit(floor_divide)/ne | solution.py:811
  1.4 1.3 %pad_add_fusion.1.place = s32[2,256]{1,0:T(2,128)} fusion(s32[1,256]{1,0:T(1,128)} %bitcast.21, s32[1,256]{1,0:T(1,128)} %bitcast.20), kind=kLoop, calls=%fused_computation.3 | loop fusion | flops 512 | bytes 4096 | tf_op jit(solution)/shard_map/stack | solution.py:807
  2.6 0.7 %broadcast_and_fusion = (s32[1,1,256]{2,1,0:T(1,128)S(1)}, s32[1,1,256]{2,1,0:T(1,128)S(1)}) fusion(s32[1,1,256]{2,1,0:T(1,128)} %param.15), kind=kLoop, calls=%fused_computation.18 | loop fusion | flops 768 | bytes 3072 | tf_op jit(solution)/shard_map/jit(remainder)/rem | solution.py:813
  3.3 0.7 %fusion.1 = (s32[256]{0:T(256)S(1)}, s32[256]{0:T(256)S(1)}) fusion(s32[256]{0:T(256)S(1)} %bitcast.18, pred[256]{0:T(512)(128)(4,1)S(1)} %compare_reduce_fusion, s32[256]{0:T(256)S(1)} %bitcast.16, s32[256]{0:T(256)} %bitcast.22), kind=kLoop, calls=%fused_computation.13 | loop fusion | flops 6144 | bytes 5376 | tf_op jit(solution)/shard_map/add | solution.py:811
  4.0 0.6 pad_add_fusion.spots
  4.6 0.0 copy-done
  4.6 0.6 dynamic-slice_bitcast_fusion.angles
  5.2 0.8 %copy.12 = s32[128,2]{1,0:T(8,128)S(1)} copy(s32[128,2]{0,1:T(2,128)} %param.14) | data formatting | bytes 2048 | tf_op args[5]
  6.0 0.7 reshape.37.corner
  6.7 18.6 %first_step.1 = (f32[3,1024,128]{2,1,0:T(8,128)}, f32[3,1024,128]{2,1,0:T(8,128)}, f32[9,32,128]{2,1,0:T(8,128)}, bf16[2,256,2048]{2,1,0:T(8,128)(2,1)}, bf16[2,...) custom-call(f32[4]{0:T(128)} %omega.3, s32[2,512]{1,0:T(2,128)} %dynamic-slice_bitcast_fusion.angles, ...), custom_call_target="tpu_custom_call" | custom-call | tf_op jit(solution)/shard_map/first_step/pallas_call | solution.py:774
  25.3 9.2 %patches.1 = (f32[3,1024,128]{2,1,0:T(8,128)}, f32[3,1024,128]{2,1,0:T(8,128)}, f32[16,256]{1,0:T(8,128)}) custom-call(s32[128]{0:T(128)} %owner.1, s32[256]{0:T(256)} %reshape.37.corner, s32[768]{0:T(1024)} %pad_add_fusion.spots, s32[2,256]{1,0:T(2,128)} %pad_add_fusion.1.place, f32[9,32,128]{2,1,0:T(8,128)} %get-tuple-element.13.halo, ...), custom_call_target="tpu_custom_call" | custom-call | tf_op jit(solution)/shard_map/patches/pallas_call | solution.py:814
  34.5 30.9 %projection.1 = f32[32,48]{1,0:T(8,128)} custom-call(f32[4]{0:T(128)} %omega.3, f32[16,256]{1,0:T(8,128)} %get-tuple-element.18.sampled, bf16[2,256,2048]{2,1,0:T(8,128)(2,1)} %get-tuple-element.19.ta_in, bf16[2,128,2048]{2,1,0:T(8,128)(2,1)} %get-tuple-element.20.tc_in, f32[2,40,2048]{2,1,0:T(8,128)} %get-tuple-element.21.tb_in, ...), custom_call_target="tpu_custom_call" | custom-call | tf_op jit(solution)/shard_map/projection/pallas_call | solution.py:830
  65.4 1.3 %copy.14 = f32[32,48]{1,0:T(8,128)} copy(f32[32,48]{1,0:T(8,128)} %projection.1) | data formatting | bytes 12288
  (1 shorter events, 0.0 us)
Async XLA Ops:
  0.6 4.0 %copy-start = (s32[4096,2]{0,1:T(2,128)S(1)}, s32[4096,2]{0,1:T(2,128)}, u32[]{:S(2)}) copy-start(s32[4096,2]{0,1:T(2,128)} %param.17) | copy-start | bytes 98308

commit v3 on v2

--- a/solution.py
+++ b/solution.py
@@ -174,7 +174,7 @@
 
 
 def directions(omega, angles, kdir):
-    index = angles[...].astype(F32)
+    index = angles[:, pl.ds(pl.multiple_of(lax.axis_index("gx") * QN, QN), QN)].astype(F32)
     theta = math.pi * (index[0:1] + 0.5) / NTH
     phi = 2.0 * math.pi * (index[1:2] + 0.5) / NPH
     st, ct = jnp.sin(theta), jnp.cos(theta)
@@ -210,7 +210,7 @@
         tb[k, CB : CB + 8, lanes] = v
 
 
-def first_kernel(omega, angles, e_in, h_in, c_in, e_out, h_out, halo2, ta_out, tc_out, tb_out, tcf_out, kdir, ta, tc, tb, tcf, es, hs, cs, ye, yh, sent, halo1, local_sem, send_sem, recv_sem):
+def first_kernel(omega, angles, points, faces, e_in, h_in, c_in, e_out, h_out, halo2, ta_out, tc_out, tb_out, tcf_out, spots, kdir, ta, tc, tb, tcf, es, hs, cs, ye, yh, sent, halo1, local_sem, send_sem, recv_sem):
     loads = [
         pltpu.make_async_copy(e_in, es.at[:, pl.ds(0, ROWS)], local_sem.at[0]),
         pltpu.make_async_copy(h_in, hs.at[:, pl.ds(CB, ROWS)], local_sem.at[1]),
@@ -222,6 +222,13 @@
     for device in neighbours():
         pl.semaphore_signal(barrier, inc=1, device_id=device, device_id_type=MESH)
     directions(omega, angles, kdir)
+    cell = jnp.maximum(points[...], 0)
+    normal = lax.shift_right_logical(faces[...], 1)
+    row = lax.shift_right_logical(cell, 7)
+    spots[0:1] = cell & (CZ - 1)
+    spots[1:2] = jnp.where(normal == 2, 0, normal + 1) * (ROWS + CB) + row
+    spots[2:3] = jnp.where(normal == 0, 2, normal - 1) * (ROWS + CB) + row
+    spots[3:8] = jnp.zeros((5, SPB), jnp.int32)
 
     def some_tables(low, high):
         def one(n, carry):
@@ -412,7 +419,7 @@
         hs[k, pl.ds((x0 + i + 1) * CB + y0, PB)] = h_new[k]
 
 
-def second_kernel(owner, corner, spots, place, halo, e_in, h_in, c_in, e_out, h_out, sampled, es, hs, cs, ye, yh, taken, slot_x, slot_y, count, sem):
+def second_kernel(owner, corner, spots, points, faces, halo, e_in, h_in, c_in, e_out, h_out, sampled, es, hs, cs, ye, yh, taken, slot_x, slot_y, count, sem):
     loads = [
         pltpu.make_async_copy(e_in, es.at[:, pl.ds(0, ROWS)], sem.at[0]),
         pltpu.make_async_copy(h_in, hs.at[:, pl.ds(CB, ROWS)], sem.at[1]),
@@ -423,8 +430,8 @@
     me = lax.axis_index("gx") * GY + lax.axis_index("gy")
 
     def look(n, found):
-        slot_x[found] = corner[2 * n]
-        slot_y[found] = corner[2 * n + 1]
+        slot_x[found] = corner[0, n]
+        slot_y[found] = corner[1, n]
         return jnp.minimum(found + (owner[n] == me).astype(jnp.int32), SLOTS)
 
     count[0] = lax.fori_loop(0, GX * GY, look, 0, unroll=8)
@@ -444,8 +451,8 @@
         h_rows = hs.reshape(3 * (ROWS + CB), CZ)
 
         def one(n, carry):
-            mask = lane == spots[n]
-            k1, k2 = spots[SPB + n], spots[2 * SPB + n]
+            mask = lane == spots[0, n]
+            k1, k2 = spots[1, n], spots[2, n]
             taken[pl.ds(n, 1)] = jnp.where(mask, h_rows[pl.ds(k1 + CB, 1)], 0.0)
             taken[pl.ds(n + SPB, 1)] = jnp.where(mask, h_rows[pl.ds(k2 + CB, 1)], 0.0)
             taken[pl.ds(n + 2 * SPB, 1)] = jnp.where(mask, e_rows[pl.ds(k1, 1)], 0.0)
@@ -457,8 +464,8 @@
         ones = jnp.ones((16, CZ), BF16)
         return dot_t(ones, high) + dot_t(ones, low)
 
-    slots = place[0:1]
-    face = place[1:2]
+    slots = points[...]
+    face = faces[...]
     sign = jnp.where(slots >= 0, (2 * (face % 2) - 1).astype(F32), 0.0)
     for moment in range(2):
         if moment:
@@ -770,8 +777,9 @@
         pltpu.VMEM((2, CB, CZ), F32),
     ]
     coef = e_coef.reshape(ROWS, CZ)
-    mine = lax.dynamic_slice(angle_index, (lax.axis_index("gx") * QN, 0), (QN, 2)).T
-    efield, hfield, halo, *tabled = pl.pallas_call(
+    points = surface_points.reshape(1, SPB)
+    faces = surface_faces.reshape(1, SPB)
+    efield, hfield, halo, *tabled, spots = pl.pallas_call(
         first_kernel,
         out_shape=(
             field,
@@ -781,9 +789,10 @@
             jax.ShapeDtypeStruct((2, 2 * ZF, QF), BF16),
             jax.ShapeDtypeStruct((2, CB + 8, QF), F32),
             jax.ShapeDtypeStruct((2, ZF, QF), F32),
+            jax.ShapeDtypeStruct((8, SPB), jnp.int32),
         ),
-        in_specs=[SMEM, VMEM, ANY, ANY, ANY],
-        out_specs=(ANY, ANY, VMEM, ANY, ANY, ANY, ANY),
+        in_specs=[SMEM, VMEM, VMEM, VMEM, ANY, ANY, ANY],
+        out_specs=(ANY, ANY, VMEM, ANY, ANY, ANY, ANY, VMEM),
         scratch_shapes=[
             pltpu.VMEM((8, QF), F32),
             pltpu.VMEM((2, 2 * XF, QF), BF16),
@@ -801,20 +810,11 @@
         ],
         compiler_params=pltpu.CompilerParams(collective_id=0, has_side_effects=True, vmem_limit_bytes=56 * 2**20),
         name="first_step",
-    )(omega, mine, efield.reshape(3, ROWS, CZ), hfield.reshape(3, ROWS, CZ), coef)
-    points = surface_points.reshape(SPB)
-    faces = surface_faces.reshape(SPB)
-    place = jnp.stack([points, faces])
-    cell = jnp.maximum(points, 0)
-    normal = faces // 2
-    span = ROWS + CB
-    first_row = jnp.where(normal == 2, 0, normal + 1) * span + cell // CZ
-    second_row = jnp.where(normal == 0, 2, normal - 1) * span + cell // CZ
-    spots = jnp.concatenate([cell % CZ, first_row, second_row])
+    )(omega, angle_index.T, points, faces, efield.reshape(3, ROWS, CZ), hfield.reshape(3, ROWS, CZ), coef)
     efield, hfield, sampled = pl.pallas_call(
         second_kernel,
         out_shape=(field, field, jax.ShapeDtypeStruct((16, SPB), F32)),
-        in_specs=[SMEM, SMEM, SMEM, VMEM, VMEM, ANY, ANY, ANY],
+        in_specs=[SMEM, SMEM, SMEM, VMEM, VMEM, VMEM, ANY, ANY, ANY],
         out_specs=(ANY, ANY, VMEM),
         scratch_shapes=fields
         + [
@@ -826,7 +826,7 @@
         ],
         compiler_params=pltpu.CompilerParams(vmem_limit_bytes=56 * 2**20),
         name="patches",
-    )(patch_owner, patch_corner.reshape(-1), spots, place, halo, efield, hfield, coef)
+    )(patch_owner, patch_corner.T, spots, points, faces, halo, efield, hfield, coef)
     far = pl.pallas_call(
         third_kernel,
         out_shape=jax.ShapeDtypeStruct((OWN, 48), F32),

time: 67.1 us -> 61.1 us (0.911)
  other arithmetic: 3.97 us -> 0 us
  local copies, waits for them, and re-layouts: 3.37 us -> 1.32 us
    another operation x1 -> x0, other arithmetic: 1.29 us -> none  [local(): place = jnp.stack([points, faces])]
    unnamed x4 -> x1, local copies, waits for them, and re-layouts: 2.12 us -> 1.32 us
    ne x1 -> x0, other arithmetic: 0.7 us -> none  [local(): first_row = jnp.where(normal == 2, 0, normal + 1) * span + cell // CZ]
    add x1 -> x0, other arithmetic: 0.69 us -> none  [local(): first_row = jnp.where(normal == 2, 0, normal + 1) * span + cell // CZ]
    rem x1 -> x0, other arithmetic: 0.68 us -> none  [local(): spots = jnp.concatenate([cell % CZ, first_row, second_row])]
where the time goes in v3:
time: 61.1 us; the launch traced here: 60.8 us
  Pallas kernels  58.8 us (96%)
  local copies, waits for them, and re-layouts  1.32 us (2%)
  between operations  0.65 us (1%)
    pallas_call x1, Pallas kernels, local(): pl.pallas_call(third_kernel, out_shape=jax.ShapeDtypeStruct((OWN, 48), F3...  30.5 us
    pallas_call x1, Pallas kernels, local(): pl.pallas_call(first_kernel, out_shape=(field, field, jax.ShapeDtypeStruc...  18.8 us
    pallas_call x1, Pallas kernels, local(): pl.pallas_call(second_kernel, out_shape=(field, field, jax.ShapeDtypeStru...  9.47 us
    unnamed x1, local copies, waits for them, and re-layouts  1.32 us

profile of v3, /device:TPU:27, one launch (start us, length us, event | category | flops | bytes accessed | tf_op | source)
XLA Modules:
  0.0 60.8 jit_solution(6065232993296030541)
XLA Ops:
  0.6 18.8 %first_step.1 = (f32[3,1024,128]{2,1,0:T(8,128)}, f32[3,1024,128]{2,1,0:T(8,128)}, f32[9,32,128]{2,1,0:T(8,128)}, bf16[2,256,2048]{2,1,0:T(8,128)(2,1)}, bf16[2,...) custom-call(f32[4]{0:T(128)} %omega.3, s32[2,4096]{1,0:T(2,128)} %bitcast.13, ...), custom_call_target="tpu_custom_call" | custom-call | tf_op jit(solution)/shard_map/first_step/pallas_call | solution.py:782
  19.5 9.5 %patches.1 = (f32[3,1024,128]{2,1,0:T(8,128)}, f32[3,1024,128]{2,1,0:T(8,128)}, f32[16,256]{1,0:T(8,128)}) custom-call(s32[128]{0:T(128)} %owner.1, s32[2,128]{1,0:T(2,128)} %bitcast.18, s32[8,256]{1,0:T(8,128)} %get-tuple-element.14.spots, s32[1,256]{1,0:T(1,128)} %bitcast.15, s32[1,256]{1,0:T(1,128)} %bitcast.17, f32[9,32,128]{2,1,0:T(8,128)} %get-tuple-element.15.halo, ...), custom_call_target="tpu_custom_call" | custom-call | tf_op jit(solution)/shard_map/patches/pallas_call | solution.py:814
  28.9 30.5 %projection.1 = f32[32,48]{1,0:T(8,128)} custom-call(f32[4]{0:T(128)} %omega.3, f32[16,256]{1,0:T(8,128)} %get-tuple-element.20.sampled, bf16[2,256,2048]{2,1,0:T(8,128)(2,1)} %get-tuple-element.21.ta_in, bf16[2,128,2048]{2,1,0:T(8,128)(2,1)} %get-tuple-element.22.tc_in, f32[2,40,2048]{2,1,0:T(8,128)} %get-tuple-element.23.tb_in, ...), custom_call_target="tpu_custom_call" | custom-call | tf_op jit(solution)/shard_map/projection/pallas_call | solution.py:830
  59.4 1.3 %copy.13 = f32[32,48]{1,0:T(8,128)} copy(f32[32,48]{1,0:T(8,128)} %projection.1) | data formatting | bytes 12288

commit v4 on v3

--- a/solution.py
+++ b/solution.py
@@ -23,6 +23,7 @@
 QN = ANG // GX
 QF = QN * FREQ
 OWN = ANG // (GX * GY)
+HALF = OWN // 2
 MESH = pl.DeviceIdType.MESH
 F32 = jnp.float32
 BF16 = jnp.bfloat16
@@ -90,6 +91,46 @@
     corner = jnp.where(last_row, halo[8, 8:9] * (0.5 * x_high), 0.0)
     yh[0] = y_low * (halo[6] - 0.5 * es[2, pl.ds(0, CB, stride=CB)])
     yh[1] = y_low * (halo[7] + 0.5 * es[0, pl.ds(0, CB, stride=CB)] - corner)
+
+
+def add_halo(es, hs, cs, halo, own):
+    gx = lax.axis_index("gx")
+    gy = lax.axis_index("gy")
+    x_low = (gx > 0).astype(F32)
+    x_high = (gx < GX - 1).astype(F32)
+    y_low = (gy > 0).astype(F32)
+    y_high = (gy < GY - 1).astype(F32)
+    last_row = rows_of((CB, CZ)) == CB - 1
+    low_rows = pl.ds(0, CB, stride=CB)
+    high_rows = pl.ds(CB - 1, CB, stride=CB)
+    h_rows = pl.ds(2 * CB - 1, CB, stride=CB)
+    plane = slice(ROWS - CB, ROWS)
+    dy, dz = 0.5 * x_high * halo[1], -0.5 * x_high * halo[0]
+    hs[1, ROWS : ROWS + CB] += dy
+    hs[2, ROWS : ROWS + CB] += dz
+    c = cs[plane]
+    es[0, plane] += c * (dz - y_prev(dz, 0.0) - dy + z_prev(dy))
+    es[1, plane] -= c * dz
+    es[2, plane] += c * dy
+    dx, dz = -0.5 * y_high * halo[5], 0.5 * y_high * halo[4]
+    hs[0, h_rows] = hs[0, h_rows] + dx
+    hs[2, h_rows] = hs[2, h_rows] + dz
+    c = cs[high_rows]
+    es[0, high_rows] = es[0, high_rows] + c * dz
+    es[1, high_rows] = es[1, high_rows] + c * (dx - z_prev(dx) - dz + y_prev(dz, 0.0))
+    es[2, high_rows] = es[2, high_rows] - c * dx
+    corner = jnp.where(last_row, halo[8, 0:1] * (0.5 * y_high), 0.0)
+    before_y = x_low * (halo[2] + 0.5 * own[1])
+    before_z = x_low * (halo[3] - 0.5 * own[0] + corner)
+    c = cs[0:CB]
+    es[1, 0:CB] += c * before_z
+    es[2, 0:CB] -= c * before_y
+    corner = jnp.where(last_row, halo[8, 8:9] * (0.5 * x_high), 0.0)
+    before_x = y_low * (halo[6] - 0.5 * own[5])
+    before_z = y_low * (halo[7] + 0.5 * own[4] - corner)
+    c = cs[low_rows]
+    es[0, low_rows] = es[0, low_rows] - c * before_z
+    es[2, low_rows] = es[2, low_rows] + c * before_x
 
 
 def advance(es, hs, cs, ye, yh):
@@ -187,7 +228,7 @@
         kdir[2:3, lanes] = ct * w
 
 
-def tables(kdir, ta, tc, tb, tcf, n):
+def tables(kdir, ta, tc, tb, n):
     y_start = (lax.axis_index("gy") * CB).astype(F32) + (0.5 - CB * GY / 2.0)
     lanes = pl.ds(pl.multiple_of(n * CHUNK, CHUNK), CHUNK)
     kx, ky, kz = kdir[0:1, lanes], kdir[1:2, lanes], kdir[2:3, lanes]
@@ -202,7 +243,6 @@
             high, low = split(v)
             tc[k, j : j + 16, lanes] = high
             tc[k, ZF + j : ZF + j + 16, lanes] = low
-            tcf[k, j : j + 16, lanes] = v
     for j in range(0, CB, 16):
         for k, v in enumerate(turn((count + (y_start + j)) * ky)):
             tb[k, j : j + 16, lanes] = v
@@ -210,7 +250,7 @@
         tb[k, CB : CB + 8, lanes] = v
 
 
-def first_kernel(omega, angles, points, faces, e_in, h_in, c_in, e_out, h_out, halo2, ta_out, tc_out, tb_out, tcf_out, spots, kdir, ta, tc, tb, tcf, es, hs, cs, ye, yh, sent, halo1, local_sem, send_sem, recv_sem):
+def first_kernel(omega, angles, points, faces, e_in, h_in, c_in, e_out, h_out, halo2, ta_out, tc_out, tb_out, spots, kdir, ta, tc, tb, es, hs, cs, ye, yh, sent, halo1, local_sem, send_sem, recv_sem):
     loads = [
         pltpu.make_async_copy(e_in, es.at[:, pl.ds(0, ROWS)], local_sem.at[0]),
         pltpu.make_async_copy(h_in, hs.at[:, pl.ds(CB, ROWS)], local_sem.at[1]),
@@ -232,7 +272,7 @@
 
     def some_tables(low, high):
         def one(n, carry):
-            tables(kdir, ta, tc, tb, tcf, n)
+            tables(kdir, ta, tc, tb, n)
             return carry
 
         lax.fori_loop(low, high, one, 0)
@@ -259,12 +299,17 @@
     prepare(es, hs, sent.at[0])
     pl.semaphore_wait(barrier, 6)
     copies = exchange(0, halo1)
+    for k in (1, 2):
+        es[k, ROWS : ROWS + CB] = jnp.zeros((CB, CZ), F32)
+        hs[k, 0:CB] = jnp.zeros((CB, CZ), F32)
+    ye[...] = jnp.zeros_like(ye)
+    yh[...] = jnp.zeros_like(yh)
+    loads[2].wait()
+    advance(es, hs, cs, ye, yh)
     some_tables(CUT1, CUT2)
-    loads[2].wait()
     for copy in copies:
         copy.wait()
-    place_halo(es, hs, halo1, ye, yh)
-    advance(es, hs, cs, ye, yh)
+    add_halo(es, hs, cs, halo1, sent.at[0])
     prepare(es, hs, sent.at[1])
     copies = exchange(1, halo2)
     stores = [
@@ -274,7 +319,7 @@
     for copy in stores:
         copy.start()
     some_tables(CUT2, QF // CHUNK)
-    for n, (table, out) in enumerate(((ta, ta_out), (tc, tc_out), (tb, tb_out), (tcf, tcf_out))):
+    for n, (table, out) in enumerate(((ta, ta_out), (tc, tc_out), (tb, tb_out))):
         copy = pltpu.make_async_copy(table, out, local_sem.at[2 + n])
         copy.start()
         stores.append(copy)
@@ -495,7 +540,7 @@
         copy.wait()
 
 
-def third_kernel(omega, sampled, ta_in, tc_in, tb_in, tcf_in, far, got, gathered, ta, tc, tb, tcf, hot, hotz, spread_hi, spread_lo, lhs1, lhs2, lhsz, acc, rows48, send_buf, recv_buf, load_sem, send1, recv1, send2, recv2):
+def third_kernel(omega, sampled, ta_in, tc_in, tb_in, far, got, gathered, ta, tc, tb, tcf, hot, hotz, spread_hi, spread_lo, lhs1, lhs2, lhsz, acc, rows48, send_buf, recv_buf, load_sem, send1, recv1, send2, recv2):
     gx = lax.axis_index("gx")
     gy = lax.axis_index("gy")
     loads = [
@@ -503,7 +548,6 @@
         pltpu.make_async_copy(tc_in, tc.at[:, pl.ds(0, 2 * ZF)], load_sem.at[1]),
         pltpu.make_async_copy(tc_in.at[:, pl.ds(0, ZF)], tc.at[:, pl.ds(2 * ZF, ZF)], load_sem.at[2]),
         pltpu.make_async_copy(tb_in, tb, load_sem.at[3]),
-        pltpu.make_async_copy(tcf_in, tcf, load_sem.at[4]),
     ]
     for copy in loads:
         copy.start()
@@ -527,6 +571,9 @@
         copy.start()
         first.append(copy)
     gathered[0] = sampled[...]
+    for copy in loads:
+        copy.wait()
+    tcf[...] = tc[:, 0:ZF].astype(F32) + tc[:, ZF : 2 * ZF].astype(F32)
     for copy in first:
         copy.wait()
 
@@ -553,18 +600,16 @@
                 to[j : j + 16, there] = jnp.where(same, 1.0, 0.0).astype(BF16)
                 to[count + j : count + j + 16, there] = jnp.where(same, sign, 0.0).astype(BF16)
 
-    def halves(v):
-        high = v.astype(BF16).astype(F32)
-        return high, v - high
-
     def spread(v, key, start, step, first_row, there, count):
-        high, low = halves(v)
+        high, low = split(v)
+        key = key.astype(BF16)
+        zero = jnp.zeros_like(high)
 
         def one(n, carry):
-            same = key == (start + step * n).astype(F32)
+            same = key == jnp.full((16, SPB), (start + step * n).astype(F32), F32).astype(BF16)
             at = pl.ds(pl.multiple_of(first_row + n * 16, 16), 16)
-            spread_hi[at, there] = jnp.where(same, high, 0.0).astype(BF16)
-            spread_lo[at, there] = jnp.where(same, low, 0.0).astype(BF16)
+            spread_hi[at, there] = jnp.where(same, high, zero)
+            spread_lo[at, there] = jnp.where(same, low, zero)
             return carry
 
         lax.fori_loop(0, count, one, 0, unroll=8)
@@ -658,9 +703,6 @@
     zero8 = jnp.zeros((8, CHUNK), F32)
     one_hot(hot, 12, 13, XF, every)
     one_hot(hotz, 14, 15, ZF, ends)
-    for copy in loads:
-        copy.wait()
-
     @pl.when(jnp.logical_not(edge))
     def _():
         spread_z(0, CB)
@@ -739,13 +781,17 @@
                 rows48[12 * f + 6 * k + j : 12 * f + 6 * k + j + 1] = v
     rows48[48:128] = jnp.zeros((80, QN), F32)
     for t in range(0, QN, 128):
-        send_buf[t : t + 128] = jnp.transpose(rows48[:, t : t + 128])
+        turned = jnp.transpose(rows48[:, t : t + 128])
+        for q in range(0, 128, OWN):
+            at = (t + q) // 2
+            second_half = pltpu.roll(turned[q + HALF : q + OWN], 64, 1)
+            send_buf[at : at + HALF] = turned[q : q + HALF] + second_half
 
     second = []
     for d in range(1, GY):
         to = lax.rem(gy + d, GY)
         copy = pltpu.make_async_remote_copy(
-            src_ref=send_buf.at[pl.ds(pl.multiple_of(to * OWN, OWN), OWN)],
+            src_ref=send_buf.at[pl.ds(pl.multiple_of(to * HALF, HALF), HALF)],
             dst_ref=recv_buf.at[GY - d],
             send_sem=send2.at[d],
             recv_sem=recv2.at[GY - d],
@@ -754,12 +800,13 @@
         )
         copy.start()
         second.append(copy)
-    total = send_buf[pl.ds(pl.multiple_of(gy * OWN, OWN), OWN)]
+    total = send_buf[pl.ds(pl.multiple_of(gy * HALF, HALF), HALF)]
     for copy in second:
         copy.wait()
     for d in range(1, GY):
         total = total + recv_buf[d]
-    far[...] = total[:, 0:48]
+    far[0:HALF] = total[:, 0:48]
+    far[HALF:OWN] = pltpu.roll(total, 64, 1)[:, 0:48]
 
 
 VMEM = pl.BlockSpec(memory_space=pltpu.VMEM)
@@ -788,17 +835,15 @@
             jax.ShapeDtypeStruct((2, 2 * XF, QF), BF16),
             jax.ShapeDtypeStruct((2, 2 * ZF, QF), BF16),
             jax.ShapeDtypeStruct((2, CB + 8, QF), F32),
-            jax.ShapeDtypeStruct((2, ZF, QF), F32),
             jax.ShapeDtypeStruct((8, SPB), jnp.int32),
         ),
         in_specs=[SMEM, VMEM, VMEM, VMEM, ANY, ANY, ANY],
-        out_specs=(ANY, ANY, VMEM, ANY, ANY, ANY, ANY, VMEM),
+        out_specs=(ANY, ANY, VMEM, ANY, ANY, ANY, VMEM),
         scratch_shapes=[
             pltpu.VMEM((8, QF), F32),
             pltpu.VMEM((2, 2 * XF, QF), BF16),
             pltpu.VMEM((2, 2 * ZF, QF), BF16),
             pltpu.VMEM((2, CB + 8, QF), F32),
-            pltpu.VMEM((2, ZF, QF), F32),
         ]
         + fields
         + [
@@ -830,7 +875,7 @@
     far = pl.pallas_call(
         third_kernel,
         out_shape=jax.ShapeDtypeStruct((OWN, 48), F32),
-        in_specs=[SMEM, VMEM, ANY, ANY, ANY, ANY],
+        in_specs=[SMEM, VMEM, ANY, ANY, ANY],
         out_specs=VMEM,
         scratch_shapes=[
             pltpu.VMEM((16, GX * SPB), F32),
@@ -848,15 +893,15 @@
             pltpu.VMEM((2, CB * 16, 4 * ZF), BF16),
             pltpu.VMEM((3, 2, 16, QF), F32),
             pltpu.VMEM((128, QN), F32),
-            pltpu.VMEM((QN, 128), F32),
-            pltpu.VMEM((GY, OWN, 128), F32),
-            pltpu.SemaphoreType.DMA((5,)),
+            pltpu.VMEM((QN // 2, 128), F32),
+            pltpu.VMEM((GY, HALF, 128), F32),
+            pltpu.SemaphoreType.DMA((4,)),
             pltpu.SemaphoreType.DMA((GX,)),
             pltpu.SemaphoreType.DMA((GX,)),
             pltpu.SemaphoreType.DMA((GY,)),
             pltpu.SemaphoreType.DMA((GY,)),
         ],
-        compiler_params=pltpu.CompilerParams(collective_id=1, has_side_effects=True, vmem_limit_bytes=56 * 2**20),
+        compiler_params=pltpu.CompilerParams(collective_id=1, has_side_effects=True, vmem_limit_bytes=44 * 2**20),
         name="projection",
     )(omega, sampled, *tabled)
     shape = (3, CB, CB, CZ)

time: 61.1 us -> 59.6 us (0.975)
  the two profiles are of different devices: /device:TPU:27 before, /device:TPU:1 now
where the time goes in v4:
time: 59.6 us; the launch traced here: 59.3 us
  Pallas kernels  57.3 us (96%)
  local copies, waits for them, and re-layouts  1.34 us (2%)
  between operations  0.73 us (1%)
    pallas_call x1, Pallas kernels, local(): pl.pallas_call(third_kernel, out_shape=jax.ShapeDtypeStruct((OWN, 48), F3...  25.8 us
    pallas_call x1, Pallas kernels, local(): pl.pallas_call(first_kernel, out_shape=(field, field, jax.ShapeDtypeStruc...  21.7 us
    pallas_call x1, Pallas kernels, local(): pl.pallas_call(second_kernel, out_shape=(field, field, jax.ShapeDtypeStru...  9.74 us
    unnamed x11, local copies, waits for them, and re-layouts  1.34 us

profile of v4, /device:TPU:1, one launch (start us, length us, event | category | flops | bytes accessed | tf_op | source)
XLA Modules:
  0.0 59.3 jit_solution(7759200647864402617)
XLA Ops:
  0.6 21.7 %first_step.1 = (f32[3,1024,128]{2,1,0:T(8,128)}, f32[3,1024,128]{2,1,0:T(8,128)}, f32[9,32,128]{2,1,0:T(8,128)}, bf16[2,256,2048]{2,1,0:T(8,128)(2,1)}, bf16[2,...) custom-call(f32[4]{0:T(128)} %omega.3, s32[2,4096]{1,0:T(2,128)} %bitcast.13, s32[1,256]{1,0:T(1,128)} %bitcast.14, ...), custom_call_target="tpu_custom_call" | custom-call | tf_op jit(solution)/shard_map/first_step/pallas_call | solution.py:829
  22.4 0.0 copy-start
  22.4 0.0 copy-start.1
  22.4 0.0 copy-start.2
  22.4 0.0 copy-start.4
  22.4 9.7 %patches.1 = (f32[3,1024,128]{2,1,0:T(8,128)}, f32[3,1024,128]{2,1,0:T(8,128)}, f32[16,256]{1,0:T(8,128)}) custom-call(s32[128]{0:T(128)} %owner.1, s32[2,128]{1,0:T(2,128)} %bitcast.18, s32[8,256]{1,0:T(8,128)} %get-tuple-element.13.spots, s32[1,256]{1,0:T(1,128)} %bitcast.15, s32[1,256]{1,0:T(1,128)} %bitcast.17, f32[9,32,128]{2,1,0:T(8,128)} %get-tuple-element.14.halo, ...), custom_call_target="tpu_custom_call" | custom-call | tf_op jit(solution)/shard_map/patches/pallas_call | solution.py:859
  32.2 0.0 copy-done
  32.2 0.0 copy-done.1
  32.2 0.0 copy-done.2
  32.2 0.0 copy-done.4
  32.2 0.0 copy-start.3
  32.2 0.7 %copy-done.3 = f32[16,256]{1,0:T(8,128)S(1)} copy-done((f32[16,256]{1,0:T(8,128)S(1)}, f32[16,256]{1,0:T(8,128)}, u32[]{:S(2)}) %copy-start.3) | copy-done | bytes 16408
  32.9 25.8 %projection.1 = f32[32,48]{1,0:T(8,128)S(1)} custom-call(f32[4]{0:T(128)S(1)} %copy-done.4, f32[16,256]{1,0:T(8,128)S(1)} %copy-done.3, bf16[2,256,2048]{2,1,0:T(8,128)(2,1)S(1)} %copy-done, bf16[2,128,2048]{2,1,0:T(8,128)(2,1)S(1)} %copy-done.1, f32[2,40,2048]{2,1,0:T(8,128)S(1)} %copy-done.2), custom_call_target="tpu_custom_call" | custom-call | tf_op jit(solution)/shard_map/projection/pallas_call | solution.py:875
  58.7 0.6 %copy.13 = f32[32,48]{1,0:T(8,128)} copy(f32[32,48]{1,0:T(8,128)S(1)} %projection.1) | data formatting | bytes 12288
Async XLA Ops:
  22.4 9.8 %copy-start = (bf16[2,256,2048]{2,1,0:T(8,128)(2,1)S(1)}, bf16[2,256,2048]{2,1,0:T(8,128)(2,1)}, u32[]{:S(2)}) copy-start(bf16[2,256,2048]{2,1,0:T(8,128)(2,1)} %get-tuple-element.20.ta_in) | copy-start | bytes 6291460
  22.4 9.8 %copy-start.1 = (bf16[2,128,2048]{2,1,0:T(8,128)(2,1)S(1)}, bf16[2,128,2048]{2,1,0:T(8,128)(2,1)}, u32[]{:S(2)}) copy-start(bf16[2,128,2048]{2,1,0:T(8,128)(2,1)} %get-tuple-element.21.tc_in) | copy-start | bytes 3145732
  22.4 9.8 %copy-start.2 = (f32[2,40,2048]{2,1,0:T(8,128)S(1)}, f32[2,40,2048]{2,1,0:T(8,128)}, u32[]{:S(2)}) copy-start(f32[2,40,2048]{2,1,0:T(8,128)} %get-tuple-element.22.tb_in) | copy-start | bytes 1966084
  22.4 9.8 %copy-start.4 = (f32[4]{0:T(128)S(1)}, f32[4]{0:T(128)}, u32[]{:S(2)}) copy-start(f32[4]{0:T(128)} %omega.3) | copy-start | bytes 52
  32.2 0.7 %copy-start.3 = (f32[16,256]{1,0:T(8,128)S(1)}, f32[16,256]{1,0:T(8,128)}, u32[]{:S(2)}) copy-start(f32[16,256]{1,0:T(8,128)} %get-tuple-element.19.sampled) | copy-start | bytes 49156

commit v5 on v4

--- a/solution.py
+++ b/solution.py
@@ -812,6 +812,7 @@
 VMEM = pl.BlockSpec(memory_space=pltpu.VMEM)
 SMEM = pl.BlockSpec(memory_space=pltpu.SMEM)
 ANY = pl.BlockSpec(memory_space=pl.ANY)
+HBM = pl.BlockSpec(memory_space=pltpu.HBM)
 
 
 def local(efield, hfield, e_coef, omega, patch_owner, patch_corner, surface_points, surface_faces, angle_index):
@@ -823,9 +824,10 @@
         pltpu.VMEM((2, CB, CZ), F32),
         pltpu.VMEM((2, CB, CZ), F32),
     ]
-    coef = e_coef.reshape(ROWS, CZ)
-    points = surface_points.reshape(1, SPB)
-    faces = surface_faces.reshape(1, SPB)
+    coef = pltpu.with_memory_space_constraint(e_coef.reshape(ROWS, CZ), pltpu.HBM)
+    omega = pltpu.with_memory_space_constraint(omega, pltpu.HBM)
+    points = pltpu.with_memory_space_constraint(surface_points.reshape(1, SPB), pltpu.HBM)
+    faces = pltpu.with_memory_space_constraint(surface_faces.reshape(1, SPB), pltpu.HBM)
     efield, hfield, halo, *tabled, spots = pl.pallas_call(
         first_kernel,
         out_shape=(
@@ -837,7 +839,7 @@
             jax.ShapeDtypeStruct((2, CB + 8, QF), F32),
             jax.ShapeDtypeStruct((8, SPB), jnp.int32),
         ),
-        in_specs=[SMEM, VMEM, VMEM, VMEM, ANY, ANY, ANY],
+        in_specs=[SMEM, VMEM, VMEM, VMEM, HBM, HBM, HBM],
         out_specs=(ANY, ANY, VMEM, ANY, ANY, ANY, VMEM),
         scratch_shapes=[
             pltpu.VMEM((8, QF), F32),
@@ -853,14 +855,22 @@
             pltpu.SemaphoreType.DMA((2, 6)),
             pltpu.SemaphoreType.DMA((2, 6)),
         ],
-        compiler_params=pltpu.CompilerParams(collective_id=0, has_side_effects=True, vmem_limit_bytes=56 * 2**20),
+        compiler_params=pltpu.CompilerParams(collective_id=0, has_side_effects=True, vmem_limit_bytes=24 * 2**20),
         name="first_step",
-    )(omega, angle_index.T, points, faces, efield.reshape(3, ROWS, CZ), hfield.reshape(3, ROWS, CZ), coef)
+    )(
+        omega,
+        pltpu.with_memory_space_constraint(angle_index.T, pltpu.HBM),
+        points,
+        faces,
+        pltpu.with_memory_space_constraint(efield.reshape(3, ROWS, CZ), pltpu.HBM),
+        pltpu.with_memory_space_constraint(hfield.reshape(3, ROWS, CZ), pltpu.HBM),
+        coef,
+    )
     efield, hfield, sampled = pl.pallas_call(
         second_kernel,
         out_shape=(field, field, jax.ShapeDtypeStruct((16, SPB), F32)),
-        in_specs=[SMEM, SMEM, SMEM, VMEM, VMEM, VMEM, ANY, ANY, ANY],
-        out_specs=(ANY, ANY, VMEM),
+        in_specs=[SMEM, SMEM, SMEM, VMEM, VMEM, VMEM, ANY, ANY, HBM],
+        out_specs=(HBM, HBM, VMEM),
         scratch_shapes=fields
         + [
             pltpu.VMEM((4 * SPB, CZ), F32),
@@ -869,7 +879,7 @@
             pltpu.SMEM((1,), jnp.int32),
             pltpu.SemaphoreType.DMA((3,)),
         ],
-        compiler_params=pltpu.CompilerParams(vmem_limit_bytes=56 * 2**20),
+        compiler_params=pltpu.CompilerParams(vmem_limit_bytes=24 * 2**20),
         name="patches",
     )(patch_owner, patch_corner.T, spots, points, faces, halo, efield, hfield, coef)
     far = pl.pallas_call(
@@ -901,7 +911,7 @@
             pltpu.SemaphoreType.DMA((GY,)),
             pltpu.SemaphoreType.DMA((GY,)),
         ],
-        compiler_params=pltpu.CompilerParams(collective_id=1, has_side_effects=True, vmem_limit_bytes=44 * 2**20),
+        compiler_params=pltpu.CompilerParams(collective_id=1, has_side_effects=True, vmem_limit_bytes=32 * 2**20),
         name="projection",
     )(omega, sampled, *tabled)
     shape = (3, CB, CB, CZ)

time: 59.6 us -> 55.9 us (0.938)
  Pallas kernels: 57.3 us -> 54.4 us
  local copies, waits for them, and re-layouts: 1.34 us -> 0.62 us
    pallas_call x1, Pallas kernels: 9.74 us -> 7.95 us  [local(): pl.pallas_call(second_kernel, out_shape=(field, field, jax.ShapeDtypeStru...]
    unnamed x11 -> x5, local copies, waits for them, and re-layouts: 1.34 us -> 0.62 us
    pallas_call x1, Pallas kernels: 21.7 us -> 21.1 us  [local(): pl.pallas_call(first_kernel, out_shape=(field, field, jax.ShapeDtypeStruc...]
where the time goes in v5:
time: 55.9 us; the launch traced here: 55.7 us
  Pallas kernels  54.4 us (97%)
  between operations  0.69 us (1%)
  local copies, waits for them, and re-layouts  0.62 us (1%)
    pallas_call x1, Pallas kernels, local(): pl.pallas_call(third_kernel, out_shape=jax.ShapeDtypeStruct((OWN, 48), F3...  25.3 us
    pallas_call x1, Pallas kernels, local(): pl.pallas_call(first_kernel, out_shape=(field, field, jax.ShapeDtypeStruc...  21.1 us
    pallas_call x1, Pallas kernels, local(): pl.pallas_call(second_kernel, out_shape=(field, field, jax.ShapeDtypeStru...  7.95 us

profile of v5, /device:TPU:1, one launch (start us, length us, event | category | flops | bytes accessed | tf_op | source)
XLA Modules:
  0.0 55.7 jit_solution(18331741944265525543)
XLA Ops:
  0.6 0.0 copy-start
  0.6 0.0 copy-start.1
  0.7 21.1 %first_step.1 = (f32[3,1024,128]{2,1,0:T(8,128)S(1)}, f32[3,1024,128]{2,1,0:T(8,128)S(1)}, f32[9,32,128]{2,1,0:T(8,128)S(1)}, bf16[2,256,2048]{2,1,0:T(8,128)(2,...) custom-call(f32[4]{0:T(128)} %omega.3, s32[2,4096]{1,0:T(2,128)} %bitcast.14, ...), custom_call_target="tpu_custom_call" | custom-call | tf_op jit(solution)/shard_map/first_step/pallas_call | solution.py:831
  21.7 0.0 copy-done
  21.7 0.0 copy-done.1
  21.8 8.0 %patches.1 = (f32[3,1024,128]{2,1,0:T(8,128)}, f32[3,1024,128]{2,1,0:T(8,128)}, f32[16,256]{1,0:T(8,128)S(1)}) custom-call(s32[128]{0:T(128)S(1)} %copy-done.1, s32[2,128]{1,0:T(2,128)S(1)} %bitcast.9, s32[8,256]{1,0:T(8,128)S(1)} %get-tuple-element.13.spots, s32[1,256]{1,0:T(1,128)} %bitcast.16, s32[1,256]{1,0:T(1,128)} %bitcast.18, ...), custom_call_target="tpu_custom_call" | custom-call | tf_op jit(solution)/shard_map/patches/pallas_call | solution.py:869
  29.7 25.3 %projection.1 = f32[32,48]{1,0:T(8,128)S(1)} custom-call(f32[4]{0:T(128)} %omega.3, f32[16,256]{1,0:T(8,128)S(1)} %get-tuple-element.19.sampled, bf16[2,256,2048]{2,1,0:T(8,128)(2,1)S(1)} %get-tuple-element.20.ta_in, bf16[2,128,2048]{2,1,0:T(8,128)(2,1)S(1)} %get-tuple-element.21.tc_in, f32[2,40,2048]{2,1,0:T(8,128)S(1)} %get-tuple-element.22.tb_in), custom_call_target="tpu_custom_call" | custom-call | tf_op jit(solution)/shard_map/projection/pallas_call | solution.py:885
  55.1 0.6 %copy.13 = f32[32,48]{1,0:T(8,128)} copy(f32[32,48]{1,0:T(8,128)S(1)} %projection.1) | data formatting | bytes 12288
Async XLA Ops:
  0.6 21.1 %copy-start = (s32[128,2]{0,1:T(2,128)S(1)}, s32[128,2]{0,1:T(2,128)}, u32[]{:S(2)}) copy-start(s32[128,2]{0,1:T(2,128)} %param.14) | copy-start | bytes 3076
  0.6 21.1 %copy-start.1 = (s32[128]{0:T(128)S(1)}, s32[128]{0:T(128)}, u32[]{:S(2)}) copy-start(s32[128]{0:T(128)} %owner.1) | copy-start | bytes 1540

commit v6 on v5

--- a/solution.py
+++ b/solution.py
@@ -204,8 +204,7 @@
     return lax.dot_general(a, b, (((1,), (1,)), ((), ())), preferred_element_type=F32)
 
 
-CUT1 = 2
-CUT2 = 5
+CUT2 = 2
 XF = 128
 ZF = 64
 YF_ROWS = 96
@@ -261,15 +260,6 @@
     barrier = pltpu.get_barrier_semaphore()
     for device in neighbours():
         pl.semaphore_signal(barrier, inc=1, device_id=device, device_id_type=MESH)
-    directions(omega, angles, kdir)
-    cell = jnp.maximum(points[...], 0)
-    normal = lax.shift_right_logical(faces[...], 1)
-    row = lax.shift_right_logical(cell, 7)
-    spots[0:1] = cell & (CZ - 1)
-    spots[1:2] = jnp.where(normal == 2, 0, normal + 1) * (ROWS + CB) + row
-    spots[2:3] = jnp.where(normal == 0, 2, normal - 1) * (ROWS + CB) + row
-    spots[3:8] = jnp.zeros((5, SPB), jnp.int32)
-
     def some_tables(low, high):
         def one(n, carry):
             tables(kdir, ta, tc, tb, n)
@@ -277,7 +267,6 @@
 
         lax.fori_loop(low, high, one, 0)
 
-    some_tables(0, CUT1)
     loads[0].wait()
     loads[1].wait()
 
@@ -306,7 +295,15 @@
     yh[...] = jnp.zeros_like(yh)
     loads[2].wait()
     advance(es, hs, cs, ye, yh)
-    some_tables(CUT1, CUT2)
+    directions(omega, angles, kdir)
+    cell = jnp.maximum(points[...], 0)
+    normal = lax.shift_right_logical(faces[...], 1)
+    row = lax.shift_right_logical(cell, 7)
+    spots[0:1] = cell & (CZ - 1)
+    spots[1:2] = jnp.where(normal == 2, 0, normal + 1) * (ROWS + CB) + row
+    spots[2:3] = jnp.where(normal == 0, 2, normal - 1) * (ROWS + CB) + row
+    spots[3:8] = jnp.zeros((5, SPB), jnp.int32)
+    some_tables(0, CUT2)
     for copy in copies:
         copy.wait()
     add_halo(es, hs, cs, halo1, sent.at[0])
@@ -556,7 +553,6 @@
         pl.semaphore_signal(barrier, inc=1, device_id=(lax.rem(gx + d, GX), gy), device_id_type=MESH)
     for d in range(1, GY):
         pl.semaphore_signal(barrier, inc=1, device_id=(gx, lax.rem(gy + d, GY)), device_id_type=MESH)
-    tc[:, 3 * ZF : 4 * ZF] = jnp.zeros((2, ZF, QF), BF16)
     pl.semaphore_wait(barrier, GX + GY - 2)
     first = []
     for d in range(1, GX):
@@ -571,6 +567,7 @@
         copy.start()
         first.append(copy)
     gathered[0] = sampled[...]
+    tc[:, 3 * ZF : 4 * ZF] = jnp.zeros((2, ZF, QF), BF16)
     for copy in loads:
         copy.wait()
     tcf[...] = tc[:, 0:ZF].astype(F32) + tc[:, ZF : 2 * ZF].astype(F32)
@@ -612,7 +609,7 @@
             spread_lo[at, there] = jnp.where(same, low, zero)
             return carry
 
-        lax.fori_loop(0, count, one, 0, unroll=8)
+        lax.fori_loop(0, count, one, 0, unroll=True)
 
     def row16(row, lanes):
         return jnp.broadcast_to(got[row : row + 1, lanes], (16, SPB))
@@ -723,7 +720,7 @@
             keep(1, total, lanes)
             return carry
 
-        lax.fori_loop(0, QF // CHUNK, chunk, 0)
+        lax.fori_loop(0, QF // CHUNK, chunk, 0, unroll=2)
 
     @pl.when(edge)
     def _():
@@ -745,7 +742,7 @@
             keep(2, total, lanes)
             return carry
 
-        lax.fori_loop(0, QF // CHUNK, chunk, 0)
+        lax.fori_loop(0, QF // CHUNK, chunk, 0, unroll=2)
 
     scale = 1.0 / math.sqrt(GX * GY * SPB)
     y_face = jnp.where(gy == 0, 16, 15)

time: 55.9 us -> 51.8 us (0.927)
  Pallas kernels: 54.4 us -> 49.8 us
    pallas_call x1, Pallas kernels: 25.3 us -> 20.7 us  [local(): pl.pallas_call(third_kernel, out_shape=jax.ShapeDtypeStruct((OWN, 48), F3...]
where the time goes in v6:
time: 51.8 us; the launch traced here: 51.1 us
  Pallas kernels  49.8 us (96%)
  between operations  0.69 us (1%)
  local copies, waits for them, and re-layouts  0.62 us (1%)
    pallas_call x1, Pallas kernels, local(): pl.pallas_call(first_kernel, out_shape=(field, field, jax.ShapeDtypeStruc...  21.1 us
    pallas_call x1, Pallas kernels, local(): pl.pallas_call(third_kernel, out_shape=jax.ShapeDtypeStruct((OWN, 48), F3...  20.7 us
    pallas_call x1, Pallas kernels, local(): pl.pallas_call(second_kernel, out_shape=(field, field, jax.ShapeDtypeStru...  8 us

profile of v6, /device:TPU:1, one launch (start us, length us, event | category | flops | bytes accessed | tf_op | source)
XLA Modules:
  0.0 51.1 jit_solution(10152129346708773913)
XLA Ops:
  0.6 0.0 copy-start
  0.6 0.0 copy-start.1
  0.7 21.1 %first_step.1 = (f32[3,1024,128]{2,1,0:T(8,128)S(1)}, f32[3,1024,128]{2,1,0:T(8,128)S(1)}, f32[9,32,128]{2,1,0:T(8,128)S(1)}, bf16[2,256,2048]{2,1,0:T(8,128)(2,...) custom-call(f32[4]{0:T(128)} %omega.3, s32[2,4096]{1,0:T(2,128)} %bitcast.14, ...), custom_call_target="tpu_custom_call" | custom-call | tf_op jit(solution)/shard_map/first_step/pallas_call | solution.py:828
  21.7 0.0 copy-done
  21.7 0.0 copy-done.1
  21.8 8.0 %patches.1 = (f32[3,1024,128]{2,1,0:T(8,128)}, f32[3,1024,128]{2,1,0:T(8,128)}, f32[16,256]{1,0:T(8,128)S(1)}) custom-call(s32[128]{0:T(128)S(1)} %copy-done.1, s32[2,128]{1,0:T(2,128)S(1)} %bitcast.9, s32[8,256]{1,0:T(8,128)S(1)} %get-tuple-element.13.spots, s32[1,256]{1,0:T(1,128)} %bitcast.16, s32[1,256]{1,0:T(1,128)} %bitcast.18, ...), custom_call_target="tpu_custom_call" | custom-call | tf_op jit(solution)/shard_map/patches/pallas_call | solution.py:866
  29.8 20.7 %projection.1 = f32[32,48]{1,0:T(8,128)S(1)} custom-call(f32[4]{0:T(128)} %omega.3, f32[16,256]{1,0:T(8,128)S(1)} %get-tuple-element.19.sampled, bf16[2,256,2048]{2,1,0:T(8,128)(2,1)S(1)} %get-tuple-element.20.ta_in, bf16[2,128,2048]{2,1,0:T(8,128)(2,1)S(1)} %get-tuple-element.21.tc_in, f32[2,40,2048]{2,1,0:T(8,128)S(1)} %get-tuple-element.22.tb_in), custom_call_target="tpu_custom_call" | custom-call | tf_op jit(solution)/shard_map/projection/pallas_call | solution.py:882
  50.5 0.6 %copy.13 = f32[32,48]{1,0:T(8,128)} copy(f32[32,48]{1,0:T(8,128)S(1)} %projection.1) | data formatting | bytes 12288
Async XLA Ops:
  0.6 21.1 %copy-start = (s32[128,2]{0,1:T(2,128)S(1)}, s32[128,2]{0,1:T(2,128)}, u32[]{:S(2)}) copy-start(s32[128,2]{0,1:T(2,128)} %param.14) | copy-start | bytes 3076
  0.6 21.1 %copy-start.1 = (s32[128]{0:T(128)S(1)}, s32[128]{0:T(128)}, u32[]{:S(2)}) copy-start(s32[128]{0:T(128)} %owner.1) | copy-start | bytes 1540
